TPU v7x, 32 devices: a whole 2x2x4 slice. The times are simulated.
32 devices in a mesh: groups: 2 (over y), row: 8 (over z, x), col: 2 (over core).
Axes of the slice: x: 2, y: 2, z: 4, core: 2. Of those that a mesh axis runs over, the one named last changes fastest.
Arguments:
- iterate: bfloat16 [16384, 3584], P(('groups', 'row'), 'col'), parts along dimension 0, may hold values from -6 to 6
Outputs:
- updated: bfloat16 [16384, 3584], P(('groups', 'row'), 'col'), parts along dimension 0
There are 2 independent parts, one for each index of `groups`. A program takes and returns all parts, laid end to end along the dimension named above; each array names one. Nothing has to cross between parts.
All inputs are finite; a program needn't handle non-finite values.
Results may differ from a plain program's by a relative error of at most 0.0049.
Values may be sent and summed in bfloat16 or wider, within the bound.
No kernel may reach another device: no remote copies, remote signals or barrier semaphores. Data moves between devices by JAX's collectives and lax.ppermute only.
A program may use at most 128 MiB of HBM per device.

v0:
```python
import jax
import jax.numpy as jnp
from jax import lax
from jax.sharding import PartitionSpec as P

R = 8192


coef_linear = 3.4445
coef_cubic = -4.775
coef_quintic = 2.0315


def partner_2(value, axis, stride):
    mask = 2**stride
    pairs = [(source, source ^ mask) for source in range(lax.axis_size(axis))]
    return lax.ppermute(value, axis, pairs)


def bit_value(position, bit_place):
    return jnp.right_shift(position, bit_place) & 1


def ordered_join(mine, partner, upper_side, axis_dim):
    return jnp.where(
        upper_side,
        jnp.concatenate([partner, mine], axis_dim),
        jnp.concatenate([mine, partner], axis_dim),
    )


def body(iterate):
    rows_count, half_cols = iterate.shape
    row_devices = lax.axis_size("row")
    col_devices = lax.axis_size("col")
    total_bits = row_devices.bit_length() - 1
    group_count = total_bits // 2
    outer_count = total_bits - group_count
    group_size = 1 << group_count
    group_bits = list(range(group_count))
    outer_bits = list(range(group_count, total_bits))
    position = lax.axis_index("row")
    column = lax.axis_index("col")
    group_index = jnp.int32(0)
    for level, bit_place in enumerate(group_bits):
        group_index = group_index + bit_value(position, bit_place) * (1 << level)
    full_cols = half_cols * col_devices
    slab_width = full_cols // (col_devices * group_size)
    row_group = iterate
    for bit_place in group_bits:
        partner = partner_2(row_group, "row", bit_place)
        row_group = ordered_join(row_group, partner, bit_value(position, bit_place) == 1, 0)
    row_group = lax.all_gather(row_group, "col", axis=1, tiled=True)
    slab_start = (column * group_size + group_index) * slab_width
    own_slab = lax.dynamic_slice_in_dim(row_group, slab_start, slab_width, 1)
    gram_part = lax.dot_general(
        row_group, own_slab, (((0,), (0,)), ((), ())), preferred_element_type=jnp.float32
    ) * (1.0 / R)
    for level in reversed(range(outer_count)):
        bit_place = outer_bits[level]
        middle = gram_part.shape[0] // 2
        lower_half = gram_part[:middle]
        upper_half = gram_part[middle:]
        upper_side = bit_value(position, bit_place) == 1
        sent_part = jnp.where(upper_side, lower_half, upper_half)
        kept_part = jnp.where(upper_side, upper_half, lower_half)
        gram_part = kept_part + partner_2(sent_part, "row", bit_place)
    gram_half = gram_part.astype(jnp.bfloat16)
    block_row = gram_half
    for bit_place in group_bits:
        partner = partner_2(block_row, "row", bit_place)
        block_row = ordered_join(block_row, partner, bit_value(position, bit_place) == 1, 1)
    block_row = lax.all_gather(block_row, "col", axis=1, tiled=True)
    column_slab = gram_half
    for bit_place in outer_bits:
        partner = partner_2(column_slab, "row", bit_place)
        column_slab = ordered_join(column_slab, partner, bit_value(position, bit_place) == 1, 0)
    square = jnp.dot(block_row, column_slab, preferred_element_type=jnp.float32)
    poly_block = (coef_cubic * gram_part + coef_quintic * square).astype(jnp.bfloat16)
    poly_slab = poly_block
    for bit_place in outer_bits:
        partner = partner_2(poly_slab, "row", bit_place)
        poly_slab = ordered_join(poly_slab, partner, bit_value(position, bit_place) == 1, 0)
    mixed = jnp.dot(row_group, poly_slab, preferred_element_type=jnp.float32)
    result = (coef_linear * own_slab.astype(jnp.float32) + mixed).astype(jnp.bfloat16)
    pieces = result
    for bit_place in reversed(group_bits):
        middle = pieces.shape[0] // 2
        lower_half = pieces[:middle]
        upper_half = pieces[middle:]
        upper_side = bit_value(position, bit_place) == 1
        sent_part = jnp.where(upper_side, lower_half, upper_half)
        kept_part = jnp.where(upper_side, upper_half, lower_half)
        arrival = partner_2(sent_part, "row", bit_place)
        pieces = ordered_join(kept_part, arrival, upper_side, 1)
    if group_count > 1:
        shaped = pieces.reshape((rows_count,) + (2,) * group_count + (slab_width,))
        order = (0,) + tuple(range(group_count, 0, -1)) + (group_count + 1,)
        pieces = jnp.transpose(shaped, order).reshape(rows_count, group_size * slab_width)
    return pieces


def solution(mesh):
    return jax.shard_map(
        body,
        mesh=mesh,
        in_specs=(P(("groups", "row"), "col"),),
        out_specs=P(("groups", "row"), "col"),
        check_vma=False,
    )
```

profile of v0, /device:TPU:0, one launch (start us, length us, event | category | flops | bytes accessed | tf_op | source)
XLA Modules:
  0.0 1024.8 jit_solution(8655812040386847973)
XLA Ops:
  6.5 5.9 copy.2
  12.5 2.9 collective-permute-start
  15.4 79.6 %collective-permute-done = bf16[1024,1792]{0,1:T(8,128)(2,1)} collective-permute-done((bf16[1024,1792]{0,1:T(8,128)(2,1)}, bf16[1024,1792]{0,1:T(8,128)(2,1)}, u32[]{:S(2)}, u32[]{:S(2)}) %collective-permute-start) | collective-permute-done | bytes 3670048 | tf_op jit(solution)/shard_map/ppermute | solution.py:17
  95.1 10.3 %maximum_select_fusion = bf16[2048,1792]{0,1:T(8,128)(2,1)} fusion(bf16[1024,1792]{0,1:T(8,128)(2,1)} %copy.2, bf16[1024,1792]{0,1:T(8,128)(2,1)} %collective-permute-done, pred[]{:T(512)S(6)} %eq.6), kind=kLoop, calls=%fused_computation.1 | loop fusion | flops 33030144 | bytes 14680065 | tf_op jit(solution)/shard_map/jit(_where)/select_n | solution.py:25
  105.4 28.6 %all-gather.3.cloned.1.call-done = bf16[2048,3584]{0,1:T(8,128)(2,1)} async-done(((bf16[2048,1792]{0,1:T(8,128)(2,1)}), bf16[2048,3584]{0,1:T(8,128)(2,1)}) %all-gather.3.cloned.1.call-update) | async-done | bytes 14680080 | tf_op jit(solution)/shard_map/all_gather | solution.py:53
  134.1 20.8 %convolution_multiply_fusion = f32[3584,896]{1,0:T(8,128)S(1)} fusion(bf16[2048,3584]{0,1:T(8,128)(2,1)} %all-gather.3.cloned.1.call-done, s32[]{:T(128)S(6)} %select_n.91), kind=kOutput, calls=%fused_computation | convolution fusion | flops 13156548608 | bytes 31195140 | tf_op jit(solution)/shard_map/dot_general | solution.py:56
  154.9 3.7 slice_select_fusion
  164.2 275.6 %collective-permute-done.1 = f32[1792,896]{1,0:T(8,128)} collective-permute-done((f32[1792,896]{1,0:T(8,128)}, f32[1792,896]{1,0:T(8,128)}, u32[]{:S(2)}, u32[]{:S(2)}) %collective-permute-start.1) | collective-permute-done | bytes 6422560 | tf_op jit(solution)/shard_map/ppermute | solution.py:17
  439.8 10.1 select_add_fusion
  449.8 3.4 slice_select_fusion.1
  454.0 69.7 %collective-permute-done.2 = f32[896,896]{1,0:T(8,128)S(1)} collective-permute-done((f32[896,896]{1,0:T(8,128)S(1)}, f32[896,896]{1,0:T(8,128)S(1)}, u32[]{:S(2)}, u32[]{:S(2)}) %collective-permute-start.2) | collective-permute-done | bytes 3211296 | tf_op jit(solution)/shard_map/ppermute | solution.py:17
  528.1 33.8 %collective-permute-done.3 = bf16[896,896]{1,0:T(8,128)(2,1)S(1)} collective-permute-done((bf16[896,896]{1,0:T(8,128)(2,1)S(1)}, bf16[896,896]{1,0:T(8,128)(2,1)S(1)}, u32[]{:S(2)}, u32[]{:S(2)}) %collective-permute-start.3) | collective-permute-done | bytes 1605664 | tf_op jit(solution)/shard_map/ppermute | solution.py:17
  565.9 33.5 %collective-permute-done.4 = bf16[896,896]{1,0:T(8,128)(2,1)S(1)} collective-permute-done((bf16[896,896]{1,0:T(8,128)(2,1)S(1)}, bf16[896,896]{1,0:T(8,128)(2,1)S(1)}, u32[]{:S(2)}, u32[]{:S(2)}) %collective-permute-start.4) | collective-permute-done | bytes 1605664 | tf_op jit(solution)/shard_map/ppermute | solution.py:17
  599.5 5.4 maximum_select_fusion.7
  606.6 4.0 collective-permute-start.5
  610.6 136.1 %collective-permute-done.5 = bf16[1792,896]{1,0:T(8,128)(2,1)S(1)} collective-permute-done((bf16[1792,896]{1,0:T(8,128)(2,1)S(1)}, bf16[1792,896]{1,0:T(8,128)(2,1)S(1)}, u32[]{:S(2)}, u32[]{:S(2)}) %collective-permute-start.5) | collective-permute-done | bytes 3211296 | tf_op jit(solution)/shard_map/ppermute | solution.py:17
  746.8 11.9 %add_convert_fusion.1 = bf16[896,896]{1,0:T(8,128)(2,1)S(1)} fusion(f32[896,896]{1,0:T(8,128)} %get-tuple-element.6, bf16[896,3584]{1,0:T(8,128)(2,1)} %all-gather.5.cloned.1.call-done, bf16[1792,896]{1,0:T(8,128)(2,1)} %copy-done.2, bf16[1792,896]{1,0:T(8,128)(2,1)S(1)} %collective-permute-done.5, pred[]{:T(512)S(6)} %eq.7), kind=kOutput, calls=%fused_computation.26 | convolution fusion | flops 5786697728 | bytes 17661952 | tf_op jit(solution)/shard_map/dot_general | solution.py:78
  758.8 36.7 %collective-permute-done.6 = bf16[896,896]{1,0:T(8,128)(2,1)S(1)} collective-permute-done((bf16[896,896]{1,0:T(8,128)(2,1)S(1)}, bf16[896,896]{1,0:T(8,128)(2,1)S(1)}, u32[]{:S(2)}, u32[]{:S(2)}) %collective-permute-start.6) | collective-permute-done | bytes 1605664 | tf_op jit(solution)/shard_map/ppermute | solution.py:17
  795.6 5.3 maximum_select_fusion.8
  802.1 139.0 %collective-permute-done.7 = bf16[1792,896]{1,0:T(8,128)(2,1)} collective-permute-done((bf16[1792,896]{1,0:T(8,128)(2,1)S(1)}, bf16[1792,896]{1,0:T(8,128)(2,1)}, u32[]{:S(2)}, u32[]{:S(2)}) %collective-permute-start.7) | collective-permute-done | bytes 3211296 | tf_op jit(solution)/shard_map/ppermute | solution.py:17
  941.1 23.2 %add_convert_fusion = bf16[2048,896]{0,1:T(8,128)(2,1)} fusion(bf16[2048,3584]{0,1:T(8,128)(2,1)} %all-gather.3.cloned.1.call-done, s32[]{:T(128)S(6)} %select_n.91, bf16[1792,896]{1,0:T(8,128)(2,1)S(1)} %maximum_select_fusion.8, bf16[1792,896]{1,0:T(8,128)(2,1)} %collective-permute-done.7, pred[]{:T(512)S(6)} %eq.7), kind=kOutput, calls=%fused_computation.2 | convolution fusion | flops 13189578752 | bytes 28442628 | tf_op jit(solution)/shard_map/dot_general | solution.py:84
  968.3 40.3 %collective-permute-done.8 = bf16[1024,896]{0,1:T(8,128)(2,1)S(1)} collective-permute-done((bf16[1024,896]{0,1:T(8,128)(2,1)S(1)}, bf16[1024,896]{0,1:T(8,128)(2,1)S(1)}, u32[]{:S(2)}, u32[]{:S(2)}) %collective-permute-start.8) | collective-permute-done | bytes 1835040 | tf_op jit(solution)/shard_map/ppermute | solution.py:17
  1008.7 3.4 maximum_select_fusion.5
  1012.0 5.9 copy.5
  (21 shorter events, 22.0 us)
Async XLA Ops:
  6.5 127.5 %all-gather.3.cloned.1.call-start = ((), (), s32[]{:S(2)}) async-start(), calls=%async_computation | async-start | bytes 22020096 | tf_op jit(solution)/shard_map/all_gather | solution.py:53
  12.5 82.6 %collective-permute-start = (bf16[1024,1792]{0,1:T(8,128)(2,1)}, bf16[1024,1792]{0,1:T(8,128)(2,1)}, u32[]{:S(2)}, u32[]{:S(2)}) collective-permute-start(bf16[1024,1792]{0,1:T(8,128)(2,1)} %copy.2), channel_id=1, source_target_pairs={{0,2},{2,0},{4,6},{6,4},{8,10},{10,8},{12,14},{14,12},{1,3},{3,1},... | collective-permute-start | bytes 11010056 | tf_op jit(solution)/shard_map/ppermute | solution.py:17
  105.4 641.4 %all-gather.5.cloned.1.call-start = ((), (), s32[]{:S(2)}) async-start(), calls=%async_computation.1 | async-start | bytes 9633792 | tf_op jit(solution)/shard_map/all_gather | solution.py:73
  154.9 6.6 copy-start.1
  161.5 278.2 %collective-permute-start.1 = (f32[1792,896]{1,0:T(8,128)}, f32[1792,896]{1,0:T(8,128)}, u32[]{:S(2)}, u32[]{:S(2)}) collective-permute-start(f32[1792,896]{1,0:T(8,128)} %slice_select_fusion), channel_id=1, source_target_pairs={{0,8},{2,10},{4,12},{6,14},{8,0},{10,2},{12,4},{14,6},{1,9},{3,11}... | collective-permute-start | bytes 19267592 | tf_op jit(solution)/shard_map/ppermute | solution.py:17
  449.8 73.8 %copy-start = (f32[1792,896]{1,0:T(8,128)S(1)}, f32[1792,896]{1,0:T(8,128)}, u32[]{:S(2)}) copy-start(f32[1792,896]{1,0:T(8,128)} %select_add_fusion) | copy-start | bytes 19267588
  453.2 70.5 %collective-permute-start.2 = (f32[896,896]{1,0:T(8,128)S(1)}, f32[896,896]{1,0:T(8,128)S(1)}, u32[]{:S(2)}, u32[]{:S(2)}) collective-permute-start(f32[896,896]{1,0:T(8,128)S(1)} %slice_select_fusion.1), channel_id=1, source_target_pairs={{0,4},{2,6},{4,0},{6,2},{8,12},{10,14},{12,8},{14,10},{1,5},{3,7},... | collective-permute-start | bytes 9633800 | tf_op jit(solution)/shard_map/ppermute | solution.py:17
  525.9 36.0 %collective-permute-start.3 = (bf16[896,896]{1,0:T(8,128)(2,1)S(1)}, bf16[896,896]{1,0:T(8,128)(2,1)S(1)}, u32[]{:S(2)}, u32[]{:S(2)}) collective-permute-start(bf16[896,896]{1,0:T(8,128)(2,1)S(1)} %get-tuple-element.5), channel_id=1, source_target_pairs={{0,2},{2,0},{4,6},{6,4},{8,10},{10,8},{12,14},{14,12},{1,3},{3,1},... | collective-permute-start | bytes 4816904 | tf_op jit(solution)/shard_map/ppermute | solution.py:17
  564.0 35.5 %collective-permute-start.4 = (bf16[896,896]{1,0:T(8,128)(2,1)S(1)}, bf16[896,896]{1,0:T(8,128)(2,1)S(1)}, u32[]{:S(2)}, u32[]{:S(2)}) collective-permute-start(bf16[896,896]{1,0:T(8,128)(2,1)S(1)} %get-tuple-element.5), channel_id=1, source_target_pairs={{0,4},{2,6},{4,0},{6,2},{8,12},{10,14},{12,8},{14,10},{1,5},{3,7},... | collective-permute-start | bytes 4816904 | tf_op jit(solution)/shard_map/ppermute | solution.py:17
  604.9 1.8 copy-start.2
  606.6 140.1 %collective-permute-start.5 = (bf16[1792,896]{1,0:T(8,128)(2,1)S(1)}, bf16[1792,896]{1,0:T(8,128)(2,1)S(1)}, u32[]{:S(2)}, u32[]{:S(2)}) collective-permute-start(bf16[1792,896]{1,0:T(8,128)(2,1)S(1)} %maximum_select_fusion.7), channel_id=1, source_target_pairs={{0,8},{2,10},{4,12},{6,14},{8,0},{10,2},{12,4},{14,6},{1,9},{3,11}... | collective-permute-start | bytes 9633800 | tf_op jit(solution)/shard_map/ppermute | solution.py:17
  758.7 36.9 %collective-permute-start.6 = (bf16[896,896]{1,0:T(8,128)(2,1)S(1)}, bf16[896,896]{1,0:T(8,128)(2,1)S(1)}, u32[]{:S(2)}, u32[]{:S(2)}) collective-permute-start(bf16[896,896]{1,0:T(8,128)(2,1)S(1)} %add_convert_fusion.1), channel_id=1, source_target_pairs={{0,4},{2,6},{4,0},{6,2},{8,12},{10,14},{12,8},{14,10},{1,5},{3,7},... | collective-permute-start | bytes 4816904 | tf_op jit(solution)/shard_map/ppermute | solution.py:17
  800.9 140.2 %collective-permute-start.7 = (bf16[1792,896]{1,0:T(8,128)(2,1)S(1)}, bf16[1792,896]{1,0:T(8,128)(2,1)}, u32[]{:S(2)}, u32[]{:S(2)}) collective-permute-start(bf16[1792,896]{1,0:T(8,128)(2,1)S(1)} %maximum_select_fusion.8), channel_id=1, source_target_pairs={{0,8},{2,10},{4,12},{6,14},{8,0},{10,2},{12,4},{14,6},{1,9},{3,11}... | collective-permute-start | bytes 9633800 | tf_op jit(solution)/shard_map/ppermute | solution.py:17
  966.6 42.1 %collective-permute-start.8 = (bf16[1024,896]{0,1:T(8,128)(2,1)S(1)}, bf16[1024,896]{0,1:T(8,128)(2,1)S(1)}, u32[]{:S(2)}, u32[]{:S(2)}) collective-permute-start(bf16[1024,896]{0,1:T(8,128)(2,1)S(1)} %get-tuple-element.7), channel_id=1, source_target_pairs={{0,2},{2,0},{4,6},{6,4},{8,10},{10,8},{12,14},{14,12},{1,3},{3,1},... | collective-permute-start | bytes 5505032 | tf_op jit(solution)/shard_map/ppermute | solution.py:17
Sparse Core Ops, SparseCore 0:
  105.5 28.5 all-gather.2
  564.1 19.3 all-gather.4
where the time goes:
time: 1030 us; the launch traced here: 1020 us
  waiting for transfers between devices  873 us (85%)
  matrix products  56 us (5%)
  other arithmetic  48.1 us (5%)
  starting transfers between devices  17.7 us (2%)
  local copies, waits for them, and re-layouts  16.5 us (2%)
  between operations  13.5 us (1%)
    ppermute x9, waiting for transfers between devices, partner_2(): return lax.ppermute(value, axis, pairs)  844 us
    all_gather x1, waiting for transfers between devices, body(): row_group = lax.all_gather(row_group, 'col', axis=1, tiled=True)  28.6 us
    select_n x5, other arithmetic, ordered_join(): jnp.where(upper_side, jnp.concatenate([partner, mine], axis_dim), jnp.con...  26.4 us
    dot_general x1, matrix products, body(): mixed = jnp.dot(row_group, poly_slab, preferred_element_type=jnp.float32)  23.2 us
    dot_general x1, matrix products, body(): lax.dot_general(row_group, own_slab, (((0,), (0,)), ((), ())), preferred_...  20.8 us
  transfers between devices with their start and end apart: 11, of which 10 were waited for; matrix products, arithmetic and copies ran while one was open for 1% of the time, Pallas kernels for 0%

commit v1 on v0

v1 whole, which is shorter than its diff:
```python
import functools

import jax
import jax.numpy as jnp
from jax import lax
from jax.experimental import pallas as pl
from jax.experimental.pallas import tpu as pltpu
from jax.sharding import PartitionSpec as P

R = 8192

coef_linear = 3.4445
coef_cubic = -4.775
coef_quintic = 2.0315

PANEL = 256
RING_MOST = 16
F32 = jnp.float32
BF16 = jnp.bfloat16


def dot(a, b, ca, cb):
    return lax.dot_general(a, b, (((ca,), (cb,)), ((), ())), preferred_element_type=F32)


def packed_gram(own, panels, reach):
    width = reach * PANEL
    wrapped = jnp.concatenate([own, own[:, : width - PANEL]], 1)
    strips = []
    for i in range(panels):
        strips.append(dot(own[:, i * PANEL : (i + 1) * PANEL], wrapped[:, i * PANEL : i * PANEL + width], 0, 0))
    return jnp.concatenate(strips, 0) * (1.0 / R)


def finish_kernel(panels, reach, x_ref, d0_ref, c0_ref, d1_ref, c1_ref, o_ref, xe, ye, yf, cross):
    rows = x_ref.shape[0]
    half = panels * PANEL
    width = reach * PANEL
    part = c0_ref.shape[1]
    diag = (d0_ref, d1_ref)
    side = (c0_ref, c1_ref)

    def extend(dst, src):
        for h in range(2):
            dst[h, :, :half] = src[:, h * half : (h + 1) * half]
            dst[h, :, half:] = src[:, h * half : h * half + width - PANEL]

    def multiply(src, emit):
        for b in range(2):
            cross[:, b * part : (b + 1) * part] = dot(src[0, :, :half], side[b][...], 1, 0)

        @pl.loop(0, panels)
        def _(j):
            at = pl.multiple_of(j * PANEL, PANEL)
            here = pl.ds(at, PANEL)
            for h in range(2):
                total = dot(src[h, :, pl.ds(at, width)], diag[h][here, :], 1, 1)
                for d in range(1, reach):
                    other = pl.ds(pl.multiple_of(lax.rem(j + panels - d, panels) * PANEL, PANEL), PANEL)
                    total += dot(src[h, :, other], diag[h][other, d * PANEL : (d + 1) * PANEL], 1, 0)
                if h == 0:
                    for b in range(2):
                        total += dot(src[1, :, b * part : (b + 1) * part], side[b][here, :], 1, 1)
                else:
                    total += cross[:, here]
                emit(h, here, total)

    extend(xe, x_ref)

    def first(h, here, total):
        yf[h, :, here] = total
        ye[h, :, here] = total.astype(BF16)

    multiply(xe, first)
    for h in range(2):
        ye[h, :, half:] = ye[h, :, : width - PANEL]

    def second(h, here, total):
        linear = coef_linear * xe[h, :, here].astype(F32) + coef_cubic * yf[h, :, here]
        at = pl.multiple_of(h * half + here.start, PANEL)
        o_ref[:, pl.ds(at, PANEL)] = (linear + coef_quintic * total).astype(BF16)

    multiply(ye, second)


def finish(x, d0, c0, d1, c1, panels, reach):
    rows, cols = x.shape
    half = panels * PANEL
    extra = (reach - 1) * PANEL
    vmem = pl.BlockSpec(memory_space=pltpu.VMEM)
    return pl.pallas_call(
        functools.partial(finish_kernel, panels, reach),
        out_shape=jax.ShapeDtypeStruct((rows, cols), BF16),
        in_specs=[vmem] * 5,
        out_specs=vmem,
        scratch_shapes=[
            pltpu.VMEM((2, rows, half + extra), BF16),
            pltpu.VMEM((2, rows, half + extra), BF16),
            pltpu.VMEM((2, rows, half), F32),
            pltpu.VMEM((rows, half), F32),
        ],
        compiler_params=pltpu.CompilerParams(vmem_limit_bytes=60 * 2**20),
        cost_estimate=pl.CostEstimate(flops=4 * rows * cols * cols, bytes_accessed=2 * cols * cols, transcendentals=0),
    )(x, d0, c0, d1, c1)


def ring_exchange(blocks, count):
    order = list(range(0, count, 2)) + list(range(1, count, 2))[::-1]
    places = [order.index(r) for r in range(count)]
    place = jnp.array(places, jnp.int32)[lax.axis_index("row")]
    pairs = {}
    for turn in (1, -1):
        pairs[turn] = [(order[p], order[(p + turn) % count]) for p in range(count)]
    streams = []
    for block in blocks:
        step_rows = block.shape[0] // (2 * count)
        for turn in (1, -1):
            streams.append((block, turn, step_rows))

    def start_row(turn, step_rows, index):
        index = lax.rem(index + 4 * count, count)
        base = 0 if turn == 1 else count * step_rows
        return base + index * step_rows

    def own(stream, index):
        block, turn, step_rows = stream
        return lax.dynamic_slice_in_dim(block, start_row(turn, step_rows, index), step_rows, 0)

    held = [own(s, place - s[1]).astype(BF16) for s in streams]
    for step in range(count - 1):
        for k, s in enumerate(streams):
            turn = s[1]
            arrived = lax.ppermute(held[k], "row", pairs[turn])
            held[k] = (arrived.astype(F32) + own(s, place - turn * (step + 2))).astype(BF16)
    outs = [jnp.zeros(b.shape, BF16) for b in blocks]
    for step in range(count):
        for k, s in enumerate(streams):
            turn = s[1]
            at = start_row(turn, s[2], place - turn * step)
            outs[k // 2] = lax.dynamic_update_slice_in_dim(outs[k // 2], held[k], at, 0)
            if step < count - 1:
                held[k] = lax.ppermute(held[k], "row", pairs[turn])
    return outs


def plain_exchange(blocks):
    outs = []
    for block in blocks:
        mine = lax.psum_scatter(block.astype(BF16), "row", scatter_dimension=0, tiled=True)
        outs.append(lax.all_gather(mine, "row", axis=0, tiled=True))
    return outs


def body(iterate):
    rows, half = iterate.shape
    count = lax.axis_size("row")
    core = lax.axis_index("col")
    panels = half // PANEL
    reach = (panels + 1) // 2
    part = half // 2
    swap = [(0, 1), (1, 0)]
    first_core = core == 0

    other = lax.ppermute(iterate, "col", swap)
    diag_part = packed_gram(iterate, panels, reach)
    left = jnp.where(first_core, iterate, other)
    right = jnp.where(first_core, other, iterate)
    side_part = dot(left, lax.dynamic_slice_in_dim(right, core * part, part, 1), 0, 0) * (1.0 / R)

    if count <= RING_MOST:
        diag, side = ring_exchange([diag_part, side_part], count)
    else:
        diag, side = plain_exchange([diag_part, side_part])
    diag_other = lax.ppermute(diag, "col", swap)
    side_other = lax.ppermute(side, "col", swap)
    d0 = jnp.where(first_core, diag, diag_other)
    d1 = jnp.where(first_core, diag_other, diag)
    c0 = jnp.where(first_core, side, side_other)
    c1 = jnp.where(first_core, side_other, side)

    share = rows // 2
    at = core * share
    mine = jnp.concatenate(
        [lax.dynamic_slice_in_dim(left, at, share, 0), lax.dynamic_slice_in_dim(right, at, share, 0)], 1
    )
    done = finish(mine, d0, c0, d1, c1, panels, reach)
    keep = lax.dynamic_slice_in_dim(done, core * half, half, 1)
    send = lax.dynamic_slice_in_dim(done, (1 - core) * half, half, 1)
    got = lax.ppermute(send, "col", swap)
    return jnp.concatenate([jnp.where(first_core, keep, got), jnp.where(first_core, got, keep)], 0)


def solution(mesh):
    return jax.shard_map(
        body,
        mesh=mesh,
        in_specs=(P(("groups", "row"), "col"),),
        out_specs=P(("groups", "row"), "col"),
        check_vma=False,
    )
```

time: 1030 us -> 285 us (0.28)
  waiting for transfers between devices: 873 us -> 90.4 us
  starting transfers between devices: 17.7 us -> 60.5 us
  Pallas kernels: 0 us -> 40.7 us
  matrix products: 56 us -> 20 us
    ppermute x9 -> x60, waiting for transfers between devices: 844 us -> 90.4 us  [the longest x28 53.7 us: ring_exchange(): arrived = lax.ppermute(held[k], 'row', pairs[turn])]
    ppermute x9 -> x60, starting transfers between devices: 17.6 us -> 60.5 us  [the longest x28 29.9 us: ring_exchange(): arrived = lax.ppermute(held[k], 'row', pairs[turn])]
    pallas_call x0 -> x1, Pallas kernels: none -> 40.7 us  [finish(): pl.pallas_call(functools.partial(finish_kernel, panels, reach), out_shape...]
    dot_general x3 -> x8, matrix products: 56 us -> 20 us  [dot(): lax.dot_general(a, b, (((ca,), (cb,)), ((), ())), preferred_element_type=...]
    all_gather x2 -> x0, waiting for transfers between devices: 28.6 us -> none  [the longest x1 28.6 us: body(): row_group = lax.all_gather(row_group, 'col', axis=1, tiled=True)]
    select_n x8 -> x4, other arithmetic: 35.8 us -> 17 us  [the longest x1 6.58 us: body(): d1 = jnp.where(first_core, diag_other, diag)]
    unnamed x7 -> x8, local copies, waits for them, and re-layouts: 10.6 us -> 0.02 us
  transfers between devices with their start and end apart: 11 -> 60, of which waited for: 10 -> 44; matrix products, arithmetic and copies ran while one was open for 1% -> 25% of each run, Pallas kernels for 0% -> 0%
where the time goes in v1:
time: 285 us
  waiting for transfers between devices  90.4 us (32%)
  starting transfers between devices  60.5 us (21%)
  Pallas kernels  40.7 us (14%)
  other arithmetic  40.6 us (14%)
  local copies, waits for them, and re-layouts  20.8 us (7%)
  matrix products  20 us (7%)
  between operations  11.5 us (4%)
    ppermute x28, waiting for transfers between devices, ring_exchange(): arrived = lax.ppermute(held[k], 'row', pairs[turn])  53.7 us
    pallas_call x1, Pallas kernels, finish(): pl.pallas_call(functools.partial(finish_kernel, panels, reach), out_shape...  40.7 us
    ppermute x28, waiting for transfers between devices, ring_exchange(): held[k] = lax.ppermute(held[k], 'row', pairs[turn])  33.2 us
    ppermute x28, starting transfers between devices, ring_exchange(): arrived = lax.ppermute(held[k], 'row', pairs[turn])  29.9 us
    ppermute x28, starting transfers between devices, ring_exchange(): held[k] = lax.ppermute(held[k], 'row', pairs[turn])  29.5 us
    dot_general x8, matrix products, dot(): lax.dot_general(a, b, (((ca,), (cb,)), ((), ())), preferred_element_type=...  20 us
    dynamic_update_slice x28, local copies, waits for them, and re-layouts, ring_exchange(): outs[k // 2] = lax.dynamic_update_slice_in_dim(outs[k // 2], held[k], at, 0)  10.3 us
    convert_element_type x12, other arithmetic, ring_exchange(): (arrived.astype(F32) + own(s, place - turn * (step + 2))).astype(BF16)  8.15 us
  transfers between devices with their start and end apart: 60, of which 44 were waited for; matrix products, arithmetic and copies ran while one was open for 25% of the time, Pallas kernels for 0%

profile of v1, /device:TPU:0, one launch (start us, length us, event | category | flops | bytes accessed | tf_op | source)
XLA Modules:
  0.0 284.6 jit_solution(9417920351703997789)
XLA Ops:
  4.5 3.6 %fusion.17 = f32[1792,1024]{1,0:T(8,128)} fusion(bf16[1024,1792]{1,0:T(8,128)(2,1)} %param.2), kind=kOutput, calls=%fused_computation.32 | convolution fusion | flops 536870912 | bytes 3670016 | tf_op jit(solution)/shard_map/dot_general | solution.py:23
  8.1 3.6 %fusion.20 = f32[1792,1024]{1,0:T(8,128)} fusion(f32[1792,1024]{1,0:T(8,128)} %fusion.17, bf16[1024,1792]{1,0:T(8,128)(2,1)} %param.2), kind=kOutput, calls=%fused_computation.33 | convolution fusion | flops 536870912 | bytes 3670016 | tf_op jit(solution)/shard_map/dot_general | solution.py:23
  20.5 7.7 %broadcast_multiply_fusion = f32[1792,1024]{1,0:T(8,128)} fusion(f32[1792,1024]{1,0:T(8,128)} %fusion.30), kind=kLoop, calls=%fused_computation.7 | loop fusion | flops 1835008 | bytes 14680064 | tf_op jit(solution)/shard_map/mul | solution.py:32
  33.3 4.9 %collective-permute-done.1 = bf16[112,1024]{1,0:T(8,128)(2,1)S(1)} collective-permute-done((bf16[112,1024]{1,0:T(8,128)(2,1)S(1)}, bf16[112,1024]{1,0:T(8,128)(2,1)S(1)}, u32[]{:S(2)}, u32[]{:S(2)}) %collective-permute-start.1) | collective-permute-done | bytes 229408 | tf_op jit(solution)/shard_map/ppermute | solution.py:133
  44.4 3.6 %collective-permute-done.2 = bf16[112,1024]{1,0:T(8,128)(2,1)S(1)} collective-permute-done((bf16[112,1024]{1,0:T(8,128)(2,1)S(1)}, bf16[112,1024]{1,0:T(8,128)(2,1)S(1)}, u32[]{:S(2)}, u32[]{:S(2)}) %collective-permute-start.2) | collective-permute-done | bytes 229408 | tf_op jit(solution)/shard_map/ppermute | solution.py:133
  54.0 2.7 collective-permute-done.10
  61.8 2.7 collective-permute-done.11
  69.7 2.7 collective-permute-done.12
  81.2 3.8 %collective-permute-done.6 = bf16[112,1024]{1,0:T(8,128)(2,1)S(1)} collective-permute-done((bf16[112,1024]{1,0:T(8,128)(2,1)S(1)}, bf16[112,1024]{1,0:T(8,128)(2,1)S(1)}, u32[]{:S(2)}, u32[]{:S(2)}) %collective-permute-start.6) | collective-permute-done | bytes 229408 | tf_op jit(solution)/shard_map/ppermute | solution.py:133
  90.4 3.1 %collective-permute-done.7 = bf16[112,1024]{1,0:T(8,128)(2,1)S(1)} collective-permute-done((bf16[112,1024]{1,0:T(8,128)(2,1)S(1)}, bf16[112,1024]{1,0:T(8,128)(2,1)S(1)}, u32[]{:S(2)}, u32[]{:S(2)}) %collective-permute-start.7) | collective-permute-done | bytes 229408 | tf_op jit(solution)/shard_map/ppermute | solution.py:133
  99.4 2.7 collective-permute-start.16
  104.7 4.1 %convolution_multiply_fusion = f32[1792,896]{1,0:T(8,128)S(1)} fusion(bf16[1024,1792]{1,0:T(8,128)(2,1)S(1)} %get-tuple-element.29, bf16[1024,1792]{1,0:T(8,128)(2,1)S(1)} %get-tuple-element.30, s32[]{:T(128)S(6)} %select_n.191), kind=kOutput, calls=%fused_computation.4 | convolution fusion | flops 3289939968 | bytes 11927556 | tf_op jit(solution)/shard_map/dot_general | solution.py:23
  113.1 3.8 %collective-permute-done.30 = bf16[112,896]{1,0:T(8,128)(2,1)S(1)} collective-permute-done((bf16[112,896]{1,0:T(8,128)(2,1)S(1)}, bf16[112,896]{1,0:T(8,128)(2,1)S(1)}, u32[]{:S(2)}, u32[]{:S(2)}) %collective-permute-start.30) | collective-permute-done | bytes 200736 | tf_op jit(solution)/shard_map/ppermute | solution.py:133
  178.2 3.1 %collective-permute-done.46 = bf16[112,896]{1,0:T(8,128)(2,1)S(1)} collective-permute-done((bf16[112,896]{1,0:T(8,128)(2,1)S(1)}, bf16[112,896]{1,0:T(8,128)(2,1)S(1)}, u32[]{:S(2)}, u32[]{:S(2)}) %collective-permute-start.46) | collective-permute-done | bytes 200736 | tf_op jit(solution)/shard_map/ppermute | solution.py:142
  183.9 3.1 %collective-permute-done.48 = bf16[112,896]{1,0:T(8,128)(2,1)S(1)} collective-permute-done((bf16[112,896]{1,0:T(8,128)(2,1)S(1)}, bf16[112,896]{1,0:T(8,128)(2,1)S(1)}, u32[]{:S(2)}, u32[]{:S(2)}) %collective-permute-start.48) | collective-permute-done | bytes 200736 | tf_op jit(solution)/shard_map/ppermute | solution.py:142
  190.1 3.3 %collective-permute-done.50 = bf16[112,896]{1,0:T(8,128)(2,1)S(1)} collective-permute-done((bf16[112,896]{1,0:T(8,128)(2,1)S(1)}, bf16[112,896]{1,0:T(8,128)(2,1)S(1)}, u32[]{:S(2)}, u32[]{:S(2)}) %collective-permute-start.50) | collective-permute-done | bytes 200736 | tf_op jit(solution)/shard_map/ppermute | solution.py:142
  197.3 3.7 %collective-permute-done.52 = bf16[112,896]{1,0:T(8,128)(2,1)S(1)} collective-permute-done((bf16[112,896]{1,0:T(8,128)(2,1)S(1)}, bf16[112,896]{1,0:T(8,128)(2,1)S(1)}, u32[]{:S(2)}, u32[]{:S(2)}) %collective-permute-start.52) | collective-permute-done | bytes 200736 | tf_op jit(solution)/shard_map/ppermute | solution.py:142
  205.0 3.3 %collective-permute-done.54 = bf16[112,896]{1,0:T(8,128)(2,1)S(1)} collective-permute-done((bf16[112,896]{1,0:T(8,128)(2,1)S(1)}, bf16[112,896]{1,0:T(8,128)(2,1)S(1)}, u32[]{:S(2)}, u32[]{:S(2)}) %collective-permute-start.54) | collective-permute-done | bytes 200736 | tf_op jit(solution)/shard_map/ppermute | solution.py:142
  214.1 3.0 %collective-permute-done.57 = bf16[112,896]{1,0:T(8,128)(2,1)S(1)} collective-permute-done((bf16[112,896]{1,0:T(8,128)(2,1)S(1)}, bf16[112,896]{1,0:T(8,128)(2,1)S(1)}, u32[]{:S(2)}, u32[]{:S(2)}) %collective-permute-start.57) | collective-permute-done | bytes 200736 | tf_op jit(solution)/shard_map/ppermute | solution.py:142
  221.6 6.6 %broadcast_select_fusion = (bf16[1792,1024]{1,0:T(8,128)(2,1)}, bf16[1792,1024]{1,0:T(8,128)(2,1)}) fusion(bf16[1792,1024]{1,0:T(8,128)(2,1)} %collective-permute-done.29, bf16[1792,1024]{1,0:T(8,128)(2,1)} %constant_dynamic-update-slice_fusion.16, pred[]{:T(512)S(6)} %eq.3), kind=kLoop, calls=%fused_computation.8 | loop fusion | flops 3670016 | bytes 14680065 | tf_op jit(solution)/shard_map/jit(_where)/select_n | solution.py:177
  228.2 5.2 %broadcast_select_fusion.4 = (bf16[1792,896]{1,0:T(8,128)(2,1)}, bf16[1792,896]{1,0:T(8,128)(2,1)}) fusion(bf16[1792,896]{1,0:T(8,128)(2,1)} %collective-permute-done.58, bf16[1792,896]{1,0:T(8,128)(2,1)S(1)} %constant_dynamic-update-slice_fusion, pred[]{:T(512)S(6)} %eq.3), kind=kLoop, calls=%fused_computation.12 | loop fusion | flops 3211264 | bytes 12845057 | tf_op jit(solution)/shard_map/jit(_where)/select_n | solution.py:179
  233.4 40.7 %shard_map.28 = bf16[512,3584]{1,0:T(8,128)(2,1)} custom-call(bf16[512,3584]{1,0:T(8,128)(2,1)} %pad_maximum_fusion.x_ref, bf16[1792,1024]{1,0:T(8,128)(2,1)} %get-tuple-element.14.d0_ref, bf16[1792,896]{1,0:T(8,128)(2,1)} %get-tuple-element.32.c0_ref, bf16[1792,1024]{1,0:T(8,128)(2,1)} %get-tuple-element.13.d1_ref, bf16[1792,896]{1,0:T(8,128)(2,1)} %get-tuple-element.31.c1_ref), custom_call_target="tpu_custom_call" | custom-call | flops 26306674688 | bytes 25690112 | tf_op jit(solution)/shard_map/pallas_call | solution.py:91
  276.2 3.5 %collective-permute-done.59 = bf16[512,1792]{1,0:T(8,128)(2,1)} collective-permute-done((bf16[512,1792]{1,0:T(8,128)(2,1)S(1)}, bf16[512,1792]{1,0:T(8,128)(2,1)}, u32[]{:S(2)}, u32[]{:S(2)}) %collective-permute-start.59) | collective-permute-done | bytes 1835040 | tf_op jit(solution)/shard_map/ppermute | solution.py:189
  279.8 2.7 broadcast_select_fusion.7
  (172 shorter events, 146.0 us)
Async XLA Ops:
  0.0 102.2 %collective-permute-start = (bf16[1024,1792]{1,0:T(8,128)(2,1)}, bf16[1024,1792]{1,0:T(8,128)(2,1)}, u32[]{:S(2)}, u32[]{:S(2)}) collective-permute-start(bf16[1024,1792]{1,0:T(8,128)(2,1)} %param.2), channel_id=1, source_target_pairs={{0,1},{1,0},{2,3},{3,2},{4,5},{5,4},{6,7},{7,6},{8,9},{9,8},{10,11... | collective-permute-start | bytes 11010056 | tf_op jit(solution)/shard_map/ppermute | solution.py:164
  29.4 8.8 %collective-permute-start.1 = (bf16[112,1024]{1,0:T(8,128)(2,1)S(1)}, bf16[112,1024]{1,0:T(8,128)(2,1)S(1)}, u32[]{:S(2)}, u32[]{:S(2)}) collective-permute-start(bf16[112,1024]{1,0:T(8,128)(2,1)S(1)} %get-tuple-element.28), channel_id=1, source_target_pairs={{0,4},{4,8},{8,12},{12,14},{14,10},{10,6},{6,2},{2,0},{1,5},{5,9},... | collective-permute-start | bytes 688136 | tf_op jit(solution)/shard_map/ppermute | solution.py:133
  88.9 8.8 %collective-permute-start.14 = (bf16[112,1024]{1,0:T(8,128)(2,1)S(1)}, bf16[112,1024]{1,0:T(8,128)(2,1)S(1)}, u32[]{:S(2)}, u32[]{:S(2)}) collective-permute-start(bf16[112,1024]{1,0:T(8,128)(2,1)S(1)} %get-tuple-element.15), channel_id=1, source_target_pairs={{0,2},{4,0},{8,4},{12,8},{14,12},{10,14},{6,10},{2,6},{1,3},{5,1},... | collective-permute-start | bytes 688136 | tf_op jit(solution)/shard_map/ppermute | solution.py:133
  97.6 13.4 %collective-permute-start.15 = (bf16[112,1024]{1,0:T(8,128)(2,1)S(1)}, bf16[112,1024]{1,0:T(8,128)(2,1)S(1)}, u32[]{:S(2)}, u32[]{:S(2)}) collective-permute-start(bf16[112,1024]{1,0:T(8,128)(2,1)S(1)} %get-tuple-element.12), channel_id=1, source_target_pairs={{0,4},{4,8},{8,12},{12,14},{14,10},{10,6},{6,2},{2,0},{1,5},{5,9},... | collective-permute-start | bytes 688136 | tf_op jit(solution)/shard_map/ppermute | solution.py:142
  99.4 11.6 %collective-permute-start.16 = (bf16[112,1024]{1,0:T(8,128)(2,1)S(1)}, bf16[112,1024]{1,0:T(8,128)(2,1)S(1)}, u32[]{:S(2)}, u32[]{:S(2)}) collective-permute-start(bf16[112,1024]{1,0:T(8,128)(2,1)S(1)} %get-tuple-element.10), channel_id=1, source_target_pairs={{0,2},{4,0},{8,4},{12,8},{14,12},{10,14},{6,10},{2,6},{1,3},{5,1},... | collective-permute-start | bytes 688136 | tf_op jit(solution)/shard_map/ppermute | solution.py:142
  108.9 8.0 %collective-permute-start.30 = (bf16[112,896]{1,0:T(8,128)(2,1)S(1)}, bf16[112,896]{1,0:T(8,128)(2,1)S(1)}, u32[]{:S(2)}, u32[]{:S(2)}) collective-permute-start(bf16[112,896]{1,0:T(8,128)(2,1)S(1)} %get-tuple-element.46), channel_id=1, source_target_pairs={{0,4},{4,8},{8,12},{12,14},{14,10},{10,6},{6,2},{2,0},{1,5},{5,9},... | collective-permute-start | bytes 602120 | tf_op jit(solution)/shard_map/ppermute | solution.py:133
  111.0 10.8 %collective-permute-start.17 = (bf16[112,1024]{1,0:T(8,128)(2,1)S(1)}, bf16[112,1024]{1,0:T(8,128)(2,1)S(1)}, u32[]{:S(2)}, u32[]{:S(2)}) collective-permute-start(bf16[112,1024]{1,0:T(8,128)(2,1)S(1)} %collective-permute-done.15), channel_id=1, source_target_pairs={{0,4},{4,8},{8,12},{12,14},{14,10},{10,6},{6,2},{2,0},{1,5},{5,9},... | collective-permute-start | bytes 688136 | tf_op jit(solution)/shard_map/ppermute | solution.py:142
  111.0 10.8 %collective-permute-start.18 = (bf16[112,1024]{1,0:T(8,128)(2,1)S(1)}, bf16[112,1024]{1,0:T(8,128)(2,1)S(1)}, u32[]{:S(2)}, u32[]{:S(2)}) collective-permute-start(bf16[112,1024]{1,0:T(8,128)(2,1)S(1)} %collective-permute-done.16), channel_id=1, source_target_pairs={{0,2},{4,0},{8,4},{12,8},{14,12},{10,14},{6,10},{2,6},{1,3},{5,1},... | collective-permute-start | bytes 688136 | tf_op jit(solution)/shard_map/ppermute | solution.py:142
  117.0 9.1 %collective-permute-start.31 = (bf16[112,896]{1,0:T(8,128)(2,1)S(1)}, bf16[112,896]{1,0:T(8,128)(2,1)S(1)}, u32[]{:S(2)}, u32[]{:S(2)}) collective-permute-start(bf16[112,896]{1,0:T(8,128)(2,1)S(1)} %get-tuple-element.44), channel_id=1, source_target_pairs={{0,4},{4,8},{8,12},{12,14},{14,10},{10,6},{6,2},{2,0},{1,5},{5,9},... | collective-permute-start | bytes 602120 | tf_op jit(solution)/shard_map/ppermute | solution.py:133
  118.3 8.0 %collective-permute-start.38 = (bf16[112,896]{1,0:T(8,128)(2,1)S(1)}, bf16[112,896]{1,0:T(8,128)(2,1)S(1)}, u32[]{:S(2)}, u32[]{:S(2)}) collective-permute-start(bf16[112,896]{1,0:T(8,128)(2,1)S(1)} %get-tuple-element.43), channel_id=1, source_target_pairs={{0,2},{4,0},{8,4},{12,8},{14,12},{10,14},{6,10},{2,6},{1,3},{5,1},... | collective-permute-start | bytes 602120 | tf_op jit(solution)/shard_map/ppermute | solution.py:133
  121.8 9.2 %collective-permute-start.19 = (bf16[112,1024]{1,0:T(8,128)(2,1)S(1)}, bf16[112,1024]{1,0:T(8,128)(2,1)S(1)}, u32[]{:S(2)}, u32[]{:S(2)}) collective-permute-start(bf16[112,1024]{1,0:T(8,128)(2,1)S(1)} %collective-permute-done.17), channel_id=1, source_target_pairs={{0,4},{4,8},{8,12},{12,14},{14,10},{10,6},{6,2},{2,0},{1,5},{5,9},... | collective-permute-start | bytes 688136 | tf_op jit(solution)/shard_map/ppermute | solution.py:142
  121.8 10.1 %collective-permute-start.20 = (bf16[112,1024]{1,0:T(8,128)(2,1)S(1)}, bf16[112,1024]{1,0:T(8,128)(2,1)S(1)}, u32[]{:S(2)}, u32[]{:S(2)}) collective-permute-start(bf16[112,1024]{1,0:T(8,128)(2,1)S(1)} %collective-permute-done.18), channel_id=1, source_target_pairs={{0,2},{4,0},{8,4},{12,8},{14,12},{10,14},{6,10},{2,6},{1,3},{5,1},... | collective-permute-start | bytes 688136 | tf_op jit(solution)/shard_map/ppermute | solution.py:142
  126.4 8.9 %collective-permute-start.32 = (bf16[112,896]{1,0:T(8,128)(2,1)S(1)}, bf16[112,896]{1,0:T(8,128)(2,1)S(1)}, u32[]{:S(2)}, u32[]{:S(2)}) collective-permute-start(bf16[112,896]{1,0:T(8,128)(2,1)S(1)} %get-tuple-element.42), channel_id=1, source_target_pairs={{0,4},{4,8},{8,12},{12,14},{14,10},{10,6},{6,2},{2,0},{1,5},{5,9},... | collective-permute-start | bytes 602120 | tf_op jit(solution)/shard_map/ppermute | solution.py:133
  131.0 9.2 %collective-permute-start.21 = (bf16[112,1024]{1,0:T(8,128)(2,1)S(1)}, bf16[112,1024]{1,0:T(8,128)(2,1)S(1)}, u32[]{:S(2)}, u32[]{:S(2)}) collective-permute-start(bf16[112,1024]{1,0:T(8,128)(2,1)S(1)} %collective-permute-done.19), channel_id=1, source_target_pairs={{0,4},{4,8},{8,12},{12,14},{14,10},{10,6},{6,2},{2,0},{1,5},{5,9},... | collective-permute-start | bytes 688136 | tf_op jit(solution)/shard_map/ppermute | solution.py:142
  131.9 10.0 %collective-permute-start.22 = (bf16[112,1024]{1,0:T(8,128)(2,1)S(1)}, bf16[112,1024]{1,0:T(8,128)(2,1)S(1)}, u32[]{:S(2)}, u32[]{:S(2)}) collective-permute-start(bf16[112,1024]{1,0:T(8,128)(2,1)S(1)} %collective-permute-done.20), channel_id=1, source_target_pairs={{0,2},{4,0},{8,4},{12,8},{14,12},{10,14},{6,10},{2,6},{1,3},{5,1},... | collective-permute-start | bytes 688136 | tf_op jit(solution)/shard_map/ppermute | solution.py:142
  136.5 8.0 %collective-permute-start.33 = (bf16[112,896]{1,0:T(8,128)(2,1)S(1)}, bf16[112,896]{1,0:T(8,128)(2,1)S(1)}, u32[]{:S(2)}, u32[]{:S(2)}) collective-permute-start(bf16[112,896]{1,0:T(8,128)(2,1)S(1)} %get-tuple-element.40), channel_id=1, source_target_pairs={{0,4},{4,8},{8,12},{12,14},{14,10},{10,6},{6,2},{2,0},{1,5},{5,9},... | collective-permute-start | bytes 602120 | tf_op jit(solution)/shard_map/ppermute | solution.py:133
  140.2 9.8 %collective-permute-start.23 = (bf16[112,1024]{1,0:T(8,128)(2,1)S(1)}, bf16[112,1024]{1,0:T(8,128)(2,1)S(1)}, u32[]{:S(2)}, u32[]{:S(2)}) collective-permute-start(bf16[112,1024]{1,0:T(8,128)(2,1)S(1)} %collective-permute-done.21), channel_id=1, source_target_pairs={{0,4},{4,8},{8,12},{12,14},{14,10},{10,6},{6,2},{2,0},{1,5},{5,9},... | collective-permute-start | bytes 688136 | tf_op jit(solution)/shard_map/ppermute | solution.py:142
  141.9 9.8 %collective-permute-start.24 = (bf16[112,1024]{1,0:T(8,128)(2,1)S(1)}, bf16[112,1024]{1,0:T(8,128)(2,1)S(1)}, u32[]{:S(2)}, u32[]{:S(2)}) collective-permute-start(bf16[112,1024]{1,0:T(8,128)(2,1)S(1)} %collective-permute-done.22), channel_id=1, source_target_pairs={{0,2},{4,0},{8,4},{12,8},{14,12},{10,14},{6,10},{2,6},{1,3},{5,1},... | collective-permute-start | bytes 688136 | tf_op jit(solution)/shard_map/ppermute | solution.py:142
  150.0 9.3 %collective-permute-start.25 = (bf16[112,1024]{1,0:T(8,128)(2,1)S(1)}, bf16[112,1024]{1,0:T(8,128)(2,1)S(1)}, u32[]{:S(2)}, u32[]{:S(2)}) collective-permute-start(bf16[112,1024]{1,0:T(8,128)(2,1)S(1)} %collective-permute-done.23), channel_id=1, source_target_pairs={{0,4},{4,8},{8,12},{12,14},{14,10},{10,6},{6,2},{2,0},{1,5},{5,9},... | collective-permute-start | bytes 688136 | tf_op jit(solution)/shard_map/ppermute | solution.py:142
  151.7 9.0 %collective-permute-start.26 = (bf16[112,1024]{1,0:T(8,128)(2,1)S(1)}, bf16[112,1024]{1,0:T(8,128)(2,1)S(1)}, u32[]{:S(2)}, u32[]{:S(2)}) collective-permute-start(bf16[112,1024]{1,0:T(8,128)(2,1)S(1)} %collective-permute-done.24), channel_id=1, source_target_pairs={{0,2},{4,0},{8,4},{12,8},{14,12},{10,14},{6,10},{2,6},{1,3},{5,1},... | collective-permute-start | bytes 688136 | tf_op jit(solution)/shard_map/ppermute | solution.py:142
  159.3 13.1 %collective-permute-start.27 = (bf16[112,1024]{1,0:T(8,128)(2,1)S(1)}, bf16[112,1024]{1,0:T(8,128)(2,1)S(1)}, u32[]{:S(2)}, u32[]{:S(2)}) collective-permute-start(bf16[112,1024]{1,0:T(8,128)(2,1)S(1)} %collective-permute-done.25), channel_id=1, source_target_pairs={{0,4},{4,8},{8,12},{12,14},{14,10},{10,6},{6,2},{2,0},{1,5},{5,9},... | collective-permute-start | bytes 688136 | tf_op jit(solution)/shard_map/ppermute | solution.py:142
  160.7 12.4 %collective-permute-start.28 = (bf16[112,1024]{1,0:T(8,128)(2,1)S(1)}, bf16[112,1024]{1,0:T(8,128)(2,1)S(1)}, u32[]{:S(2)}, u32[]{:S(2)}) collective-permute-start(bf16[112,1024]{1,0:T(8,128)(2,1)S(1)} %collective-permute-done.26), channel_id=1, source_target_pairs={{0,2},{4,0},{8,4},{12,8},{14,12},{10,14},{6,10},{2,6},{1,3},{5,1},... | collective-permute-start | bytes 688136 | tf_op jit(solution)/shard_map/ppermute | solution.py:142
  173.8 47.8 %collective-permute-start.29 = (bf16[1792,1024]{1,0:T(8,128)(2,1)}, bf16[1792,1024]{1,0:T(8,128)(2,1)}, u32[]{:S(2)}, u32[]{:S(2)}) collective-permute-start(bf16[1792,1024]{1,0:T(8,128)(2,1)} %constant_dynamic-update-slice_fusion.16), channel_id=1, source_target_pairs={{0,1},{1,0},{2,3},{3,2},{4,5},{5,4},{6,7},{7,6},{8,9},{9,8},{10,11... | collective-permute-start | bytes 11010056 | tf_op jit(solution)/shard_map/ppermute | solution.py:174
  217.1 11.1 %collective-permute-start.58 = (bf16[1792,896]{1,0:T(8,128)(2,1)S(1)}, bf16[1792,896]{1,0:T(8,128)(2,1)}, u32[]{:S(2)}, u32[]{:S(2)}) collective-permute-start(bf16[1792,896]{1,0:T(8,128)(2,1)S(1)} %constant_dynamic-update-slice_fusion), channel_id=1, source_target_pairs={{0,1},{1,0},{2,3},{3,2},{4,5},{5,4},{6,7},{7,6},{8,9},{9,8},{10,11... | collective-permute-start | bytes 9633800 | tf_op jit(solution)/shard_map/ppermute | solution.py:175
  (40 other events, 260.5 us)

commit v2 on v1

v2 whole, which is shorter than its diff:
```python
import functools

import jax
import jax.numpy as jnp
from jax import lax
from jax.experimental import pallas as pl
from jax.experimental.pallas import tpu as pltpu
from jax.sharding import PartitionSpec as P

R = 8192

coef_linear = 3.4445
coef_cubic = -4.775
coef_quintic = 2.0315

PANEL = 256
RING_MOST = 16
F32 = jnp.float32
BF16 = jnp.bfloat16


def dot(a, b, ca, cb):
    return lax.dot_general(a, b, (((ca,), (cb,)), ((), ())), preferred_element_type=F32)


def diag_kernel(x_ref, o_ref, wide):
    half = x_ref.shape[1]
    width = o_ref.shape[1]
    wide[:, :half] = x_ref[...]
    wide[:, half:] = x_ref[:, : width - PANEL]
    for at in range(0, half, PANEL):
        strip = dot(x_ref[:, at : at + PANEL], wide[:, at : at + width], 0, 0)
        o_ref[at : at + PANEL, :] = (strip * (1.0 / R)).astype(BF16)


def diag_gram(x, width):
    rows, half = x.shape
    vmem = pl.BlockSpec(memory_space=pltpu.VMEM)
    return pl.pallas_call(
        diag_kernel,
        out_shape=jax.ShapeDtypeStruct((half, width), BF16),
        in_specs=[vmem],
        out_specs=vmem,
        scratch_shapes=[pltpu.VMEM((rows, half + width - PANEL), BF16)],
        compiler_params=pltpu.CompilerParams(vmem_limit_bytes=40 * 2**20),
        cost_estimate=pl.CostEstimate(flops=2 * rows * half * width, bytes_accessed=4 * rows * half, transcendentals=0),
    )(x)


def side_kernel(core_ref, own_ref, other_ref, o_ref):
    half = own_ref.shape[1]
    part = half // 2

    def go(left_ref, right_ref, start):
        for at in range(0, half, PANEL):
            strip = dot(left_ref[:, at : at + PANEL], right_ref[:, start : start + part], 0, 0)
            o_ref[at : at + PANEL, :] = (strip * (1.0 / R)).astype(BF16)

    @pl.when(core_ref[0] == 0)
    def _():
        go(own_ref, other_ref, 0)

    @pl.when(core_ref[0] == 1)
    def _():
        go(other_ref, own_ref, part)


def side_gram(core, own, other):
    rows, half = own.shape
    vmem = pl.BlockSpec(memory_space=pltpu.VMEM)
    return pl.pallas_call(
        side_kernel,
        out_shape=jax.ShapeDtypeStruct((half, half // 2), BF16),
        in_specs=[pl.BlockSpec(memory_space=pltpu.SMEM), vmem, vmem],
        out_specs=vmem,
        compiler_params=pltpu.CompilerParams(vmem_limit_bytes=40 * 2**20),
        cost_estimate=pl.CostEstimate(flops=rows * half * half, bytes_accessed=6 * rows * half, transcendentals=0),
    )(core.reshape(1), own, other)


def finish_kernel(panels, reach, part, pieces, place_ref, *refs):
    own_ref, other_ref = refs[:2]
    piece_refs = refs[2 : 2 + 2 * sum(pieces)]
    keep_ref, send_ref, xe, ye, yf, cross, diag, side, out, sems = refs[2 + 2 * sum(pieces) :]
    core = place_ref[0]
    rows = xe.shape[1]
    half = panels * PANEL
    width = reach * PANEL

    copies = []

    def bring(source, target):
        copy = pltpu.make_async_copy(source, target, sems.at[len(copies)])
        copy.start()
        copies.append(copy)

    mine = pl.ds(pl.multiple_of(core * rows, rows), rows)
    bring(own_ref.at[mine, :], xe.at[core, :, pl.ds(0, half)])
    bring(other_ref.at[mine, :], xe.at[1 - core, :, pl.ds(0, half)])
    at = 0
    for owner in (core, 1 - core):
        for k, store in enumerate((diag, side)):
            for m in range(pieces[k]):
                piece = piece_refs[at]
                start = place_ref[1 + m + (pieces[0] if k == 1 else 0)]
                start = pl.multiple_of(start, 16)
                bring(piece, store.at[owner, pl.ds(start, piece.shape[0]), :])
                at += 1
    for copy in copies:
        copy.wait()

    def multiply(src, emit):
        for b in range(2):
            cross[:, b * part : (b + 1) * part] = dot(src[0, :, :half], side[b], 1, 0)

        @pl.loop(0, panels)
        def _(j):
            at = pl.multiple_of(j * PANEL, PANEL)
            here = pl.ds(at, PANEL)
            for h in range(2):
                total = dot(src[h, :, pl.ds(at, width)], diag[h, here, :], 1, 1)
                for d in range(1, reach):
                    there = pl.ds(pl.multiple_of(lax.rem(j + panels - d, panels) * PANEL, PANEL), PANEL)
                    total += dot(src[h, :, there], diag[h, there, d * PANEL : (d + 1) * PANEL], 1, 0)
                if h == 0:
                    for b in range(2):
                        total += dot(src[1, :, b * part : (b + 1) * part], side[b, here, :], 1, 1)
                else:
                    total += cross[:, here]
                emit(h, here, total)

    for h in range(2):
        xe[h, :, half:] = xe[h, :, : width - PANEL]

    def first(h, here, total):
        yf[h, :, here] = total
        ye[h, :, here] = total.astype(BF16)

    multiply(xe, first)
    for h in range(2):
        ye[h, :, half:] = ye[h, :, : width - PANEL]

    def second(h, here, total):
        linear = coef_linear * xe[h, :, here].astype(F32) + coef_cubic * yf[h, :, here]
        out[h, :, here] = (linear + coef_quintic * total).astype(BF16)

    multiply(ye, second)
    last = [
        pltpu.make_async_copy(out.at[core], keep_ref, sems.at[0]),
        pltpu.make_async_copy(out.at[1 - core], send_ref, sems.at[1]),
    ]
    for copy in last:
        copy.start()
    for copy in last:
        copy.wait()


def finish(core, own, other, starts, mine, theirs, panels, reach):
    rows, half = own.shape
    share = rows // 2
    part = half // 2
    width = reach * PANEL
    pieces = tuple(len(p) for p in mine)
    operands = [own, other, *mine[0], *mine[1], *theirs[0], *theirs[1]]
    place = jnp.stack([core, *starts]).astype(jnp.int32)
    anywhere = pl.BlockSpec(memory_space=pl.ANY)
    return pl.pallas_call(
        functools.partial(finish_kernel, panels, reach, part, pieces),
        out_shape=[jax.ShapeDtypeStruct((share, half), BF16)] * 2,
        in_specs=[pl.BlockSpec(memory_space=pltpu.SMEM)] + [anywhere] * len(operands),
        out_specs=[anywhere] * 2,
        scratch_shapes=[
            pltpu.VMEM((2, share, half + width - PANEL), BF16),
            pltpu.VMEM((2, share, half + width - PANEL), BF16),
            pltpu.VMEM((2, share, half), F32),
            pltpu.VMEM((share, half), F32),
            pltpu.VMEM((2, half, width), BF16),
            pltpu.VMEM((2, half, part), BF16),
            pltpu.VMEM((2, share, half), BF16),
            pltpu.SemaphoreType.DMA((len(operands),)),
        ],
        compiler_params=pltpu.CompilerParams(vmem_limit_bytes=56 * 2**20),
        cost_estimate=pl.CostEstimate(flops=16 * share * half * half, bytes_accessed=8 * half * half, transcendentals=0),
    )(place, *operands)


def join_kernel(core_ref, keep_ref, got_ref, o_ref):
    core = core_ref[0]
    rows = keep_ref.shape[0]
    o_ref[pl.ds(pl.multiple_of(core * rows, rows), rows), :] = keep_ref[...]
    o_ref[pl.ds(pl.multiple_of((1 - core) * rows, rows), rows), :] = got_ref[...]


def join(core, keep, got):
    rows, cols = keep.shape
    vmem = pl.BlockSpec(memory_space=pltpu.VMEM)
    return pl.pallas_call(
        join_kernel,
        out_shape=jax.ShapeDtypeStruct((2 * rows, cols), BF16),
        in_specs=[pl.BlockSpec(memory_space=pltpu.SMEM), vmem, vmem],
        out_specs=vmem,
    )(core.reshape(1), keep, got)


def ring_exchange(blocks):
    count = lax.axis_size("row")
    order = list(range(0, count, 2)) + list(range(1, count, 2))[::-1]
    places = [order.index(r) for r in range(count)]
    place = jnp.array(places, jnp.int32)[lax.axis_index("row")]
    far = count // 2
    turns = (1, -1)
    pairs = {t: [(order[p], order[(p + t) % count]) for p in range(count)] for t in turns}
    sizes = [b.shape[0] // count for b in blocks]

    def row_of(k, distance):
        return lax.rem(place + distance + count, count) * sizes[k]

    def own(k, distance):
        return lax.dynamic_slice_in_dim(blocks[k], row_of(k, distance), sizes[k], 0)

    def half_of(value, turn):
        middle = value.shape[0] // 2
        return value[:middle] if turn == 1 else value[middle:]

    def add(a, b):
        return (a.astype(F32) + b.astype(F32)).astype(BF16)

    parts = range(len(blocks))
    held = {(k, t): half_of(own(k, far), t).astype(BF16) for k in parts for t in turns}
    for distance in range(far - 1, -1, -1):
        for k in parts:
            arrived = {t: lax.ppermute(held[k, t], "row", pairs[t]) for t in turns}
            if distance == 0:
                total = own(k, 0).astype(F32)
                total = total + arrived[1].astype(F32) + arrived[-1].astype(F32)
                held[k, 1] = held[k, -1] = total.astype(BF16)
                continue
            for t in turns:
                mine = own(k, t * distance)
                if distance == far - 1:
                    middle = mine.shape[0] // 2
                    if t == 1:
                        held[k, t] = jnp.concatenate([add(mine[:middle], arrived[t]), mine[middle:].astype(BF16)], 0)
                    else:
                        held[k, t] = jnp.concatenate([mine[:middle].astype(BF16), add(mine[middle:], arrived[t])], 0)
                else:
                    held[k, t] = add(mine, arrived[t])
    pieces = [[held[k, 1]] for k in parts]
    starts = [[row_of(k, 0)] for k in parts]
    for distance in range(1, far + 1):
        for k in parts:
            for t in turns:
                sent = held[k, t] if distance < far else half_of(held[k, t], t)
                held[k, t] = lax.ppermute(sent, "row", pairs[t])
                at = row_of(k, -t * distance)
                if distance == far and t == -1:
                    at = at + sizes[k] // 2
                pieces[k].append(held[k, t])
                starts[k].append(at)
    return pieces, starts[0] + starts[1]


def plain_exchange(blocks):
    pieces = []
    for block in blocks:
        mine = lax.psum_scatter(block, "row", scatter_dimension=0, tiled=True)
        pieces.append([lax.all_gather(mine, "row", axis=0, tiled=True)])
    return pieces, [jnp.int32(0)] * len(blocks)


def body(iterate):
    half = iterate.shape[1]
    count = lax.axis_size("row")
    core = lax.axis_index("col")
    panels = half // PANEL
    reach = (panels + 1) // 2
    swap = [(0, 1), (1, 0)]

    other = lax.ppermute(iterate, "col", swap)
    diag_part = diag_gram(iterate, reach * PANEL)
    side_part = side_gram(core, iterate, other)
    diag_part, side_part = lax.optimization_barrier((diag_part, side_part))
    exchange = ring_exchange if count <= RING_MOST else plain_exchange
    mine, starts = exchange([diag_part, side_part])
    theirs = [[lax.ppermute(piece, "col", swap) for piece in kind] for kind in mine]
    keep, send = finish(core, iterate, other, starts, mine, theirs, panels, reach)
    return join(core, keep, lax.ppermute(send, "col", swap))


def solution(mesh):
    return jax.shard_map(
        body,
        mesh=mesh,
        in_specs=(P(("groups", "row"), "col"),),
        out_specs=P(("groups", "row"), "col"),
        check_vma=False,
    )
```

time: 285 us -> 230 us (0.81)
  starting transfers between devices: 60.5 us -> 38 us
  other arithmetic: 40.6 us -> 19.5 us
  matrix products: 20 us -> 0 us
  Pallas kernels: 40.7 us -> 55.6 us
  local copies, waits for them, and re-layouts: 20.8 us -> 9.47 us
  waiting for transfers between devices: 90.4 us -> 101 us
  between operations: 11.5 us -> 6.21 us
    ppermute x59 -> x51, starting transfers between devices: 60 us -> 37.5 us  [the longest x16 18.4 us: ring_exchange(): held[k, t] = lax.ppermute(sent, 'row', pairs[t])]
    dot_general x8 -> x0, matrix products: 20 us -> none  [dot(): lax.dot_general(a, b, (((ca,), (cb,)), ((), ())), preferred_element_type=...]
    select_n x4 -> x0, other arithmetic: 17 us -> none  [the longest x1 6.58 us: body(): d1 = jnp.where(first_core, diag_other, diag)]
    pallas_call x1 -> x4, Pallas kernels: 40.7 us -> 55.6 us  [the longest x1 41.4 us: finish(): pl.pallas_call(functools.partial(finish_kernel, panels, reach, part, piec...]
    ppermute x59 -> x51, waiting for transfers between devices: 90.4 us -> 101 us  [the longest x16 52.1 us: ring_exchange(): held[k, t] = lax.ppermute(sent, 'row', pairs[t])]
    dynamic_update_slice x28 -> x0, local copies, waits for them, and re-layouts: 10.3 us -> none  [ring_exchange(): outs[k // 2] = lax.dynamic_update_slice_in_dim(outs[k // 2], held[k], at, 0)]
    convert_element_type x12 -> x10, other arithmetic: 8.15 us -> 16.9 us  [the longest x8 14.1 us: add(): return (a.astype(F32) + b.astype(F32)).astype(BF16)]
    mul x1 -> x0, other arithmetic: 7.67 us -> none  [packed_gram(): return jnp.concatenate(strips, 0) * (1.0 / R)]
  transfers between devices with their start and end apart: 60 -> 52, of which waited for: 44 -> 25; matrix products, arithmetic and copies ran while one was open for 25% -> 10% of each run, Pallas kernels for 0% -> 2%
where the time goes in v2:
time: 230 us
  waiting for transfers between devices  101 us (44%)
  Pallas kernels  55.6 us (24%)
  starting transfers between devices  38 us (17%)
  other arithmetic  19.5 us (8%)
  local copies, waits for them, and re-layouts  9.47 us (4%)
  between operations  6.21 us (3%)
    ppermute x16, waiting for transfers between devices, ring_exchange(): held[k, t] = lax.ppermute(sent, 'row', pairs[t])  52.1 us
    ppermute x16, waiting for transfers between devices, ring_exchange(): arrived = {t: lax.ppermute(held[k, t], 'row', pairs[t]) for t in turns}  43.2 us
    pallas_call x1, Pallas kernels, finish(): pl.pallas_call(functools.partial(finish_kernel, panels, reach, part, piec...  41.4 us
    ppermute x16, starting transfers between devices, ring_exchange(): held[k, t] = lax.ppermute(sent, 'row', pairs[t])  18.4 us
    ppermute x16, starting transfers between devices, ring_exchange(): arrived = {t: lax.ppermute(held[k, t], 'row', pairs[t]) for t in turns}  16.8 us
    convert_element_type x8, other arithmetic, add(): return (a.astype(F32) + b.astype(F32)).astype(BF16)  14.1 us
    pallas_call x1, Pallas kernels, side_gram(): pl.pallas_call(side_kernel, out_shape=jax.ShapeDtypeStruct((half, half //...  6.05 us
    unnamed x62, local copies, waits for them, and re-layouts  5.2 us
  transfers between devices with their start and end apart: 52, of which 25 were waited for; matrix products, arithmetic and copies ran while one was open for 10% of the time, Pallas kernels for 2%

profile of v2, /device:TPU:0, one launch (start us, length us, event | category | flops | bytes accessed | tf_op | source)
XLA Modules:
  0.0 229.7 jit_solution(12128566623212450967)
XLA Ops:
  5.7 4.0 %shard_map.28 = bf16[1792,1024]{1,0:T(8,128)(2,1)S(1)} custom-call(bf16[1024,1792]{1,0:T(8,128)(2,1)S(1)} %copy-done.1), custom_call_target="tpu_custom_call" | custom-call | flops 3758096384 | bytes 7340032 | tf_op jit(solution)/shard_map/pallas_call | solution.py:39
  11.5 6.0 %shard_map.29 = bf16[1792,896]{1,0:T(8,128)(2,1)S(1)} custom-call(s32[1]{0:T(128)} %bitcast.core_ref, bf16[1024,1792]{1,0:T(8,128)(2,1)S(1)} %copy-done.1, bf16[1024,1792]{1,0:T(8,128)(2,1)} %collective-permute-done.other_ref.refs_1_), custom_call_target="tpu_custom_call" | custom-call | flops 3288334336 | bytes 11010048 | tf_op jit(solution)/shard_map/pallas_call | solution.py:71
  18.5 2.6 %collective-permute-start.17 = (bf16[112,896]{1,0:T(8,128)(2,1)}, bf16[112,896]{1,0:T(8,128)(2,1)}, u32[]{:S(2)}, u32[]{:S(2)}) collective-permute-start(bf16[112,896]{1,0:T(8,128)(2,1)} %get-tuple-element.25), channel_id=1, source_target_pairs={{0,4},{4,8},{8,12},{12,14},{14,10},{10,6},{6,2},{2,0},{1,5},{5,9},... | collective-permute-start | bytes 602120 | tf_op jit(solution)/shard_map/ppermute | solution.py:232
  38.6 5.0 %collective-permute-done.18 = bf16[224,896]{1,0:T(8,128)(2,1)S(1)} collective-permute-done((bf16[224,896]{1,0:T(8,128)(2,1)S(1)}, bf16[224,896]{1,0:T(8,128)(2,1)S(1)}, u32[]{:S(2)}, u32[]{:S(2)}) %collective-permute-start.18) | collective-permute-done | bytes 401440 | tf_op jit(solution)/shard_map/ppermute | solution.py:232
  46.0 7.4 %collective-permute-done.2 = bf16[224,1024]{1,0:T(8,128)(2,1)S(1)} collective-permute-done((bf16[224,1024]{1,0:T(8,128)(2,1)S(1)}, bf16[224,1024]{1,0:T(8,128)(2,1)S(1)}, u32[]{:S(2)}, u32[]{:S(2)}) %collective-permute-start.2) | collective-permute-done | bytes 458784 | tf_op jit(solution)/shard_map/ppermute | solution.py:232
  58.2 3.9 %collective-permute-done.19 = bf16[224,896]{1,0:T(8,128)(2,1)} collective-permute-done((bf16[224,896]{1,0:T(8,128)(2,1)}, bf16[224,896]{1,0:T(8,128)(2,1)}, u32[]{:S(2)}, u32[]{:S(2)}) %collective-permute-start.19) | collective-permute-done | bytes 401440 | tf_op jit(solution)/shard_map/ppermute | solution.py:232
  64.3 5.3 %collective-permute-done.3 = bf16[224,1024]{1,0:T(8,128)(2,1)} collective-permute-done((bf16[224,1024]{1,0:T(8,128)(2,1)}, bf16[224,1024]{1,0:T(8,128)(2,1)}, u32[]{:S(2)}, u32[]{:S(2)}) %collective-permute-start.3) | collective-permute-done | bytes 458784 | tf_op jit(solution)/shard_map/ppermute | solution.py:232
  69.6 2.7 %add_convert_fusion.3 = (bf16[224,1024]{1,0:T(8,128)(2,1)}, bf16[224,1024]{1,0:T(8,128)(2,1)}) fusion(bf16[224,1024]{1,0:T(8,128)(2,1)} %collective-permute-done.3, bf16[1792,1024]{1,0:T(8,128)(2,1)} %copy-done, s32[]{:T(128)S(6)} %select_n.39, bf16[224,1024]{1,0:T(8,128)(2,1)} %collective-permute-done.6, s32[]{:T(128)S(6)} %select_n.44), kind=kLoop, calls=%fused_computation.3 | loop fusion | flops 1835008 | bytes 2752520 | tf_op jit(solution)/shard_map/convert_element_type | solution.py:226
  78.9 7.2 %collective-permute-done.7 = bf16[224,1024]{1,0:T(8,128)(2,1)} collective-permute-done((bf16[224,1024]{1,0:T(8,128)(2,1)}, bf16[224,1024]{1,0:T(8,128)(2,1)}, u32[]{:S(2)}, u32[]{:S(2)}) %collective-permute-start.7) | collective-permute-done | bytes 458784 | tf_op jit(solution)/shard_map/ppermute | solution.py:232
  89.7 5.0 %collective-permute-done.24 = bf16[224,896]{1,0:T(8,128)(2,1)} collective-permute-done((bf16[224,896]{1,0:T(8,128)(2,1)}, bf16[224,896]{1,0:T(8,128)(2,1)}, u32[]{:S(2)}, u32[]{:S(2)}) %collective-permute-start.24) | collective-permute-done | bytes 401440 | tf_op jit(solution)/shard_map/ppermute | solution.py:232
  98.2 5.1 %collective-permute-done.8 = bf16[224,1024]{1,0:T(8,128)(2,1)} collective-permute-done((bf16[224,1024]{1,0:T(8,128)(2,1)}, bf16[224,1024]{1,0:T(8,128)(2,1)}, u32[]{:S(2)}, u32[]{:S(2)}) %collective-permute-start.8) | collective-permute-done | bytes 458784 | tf_op jit(solution)/shard_map/ppermute | solution.py:232
  107.1 4.5 %collective-permute-done.26.refs_13_ = bf16[224,896]{1,0:T(8,128)(2,1)S(1)} collective-permute-done((bf16[224,896]{1,0:T(8,128)(2,1)S(1)}, bf16[224,896]{1,0:T(8,128)(2,1)S(1)}, u32[]{:S(2)}, u32[]{:S(2)}) %collective-permute-start.26) | collective-permute-done | bytes 401440 | tf_op jit(solution)/shard_map/ppermute | solution.py:254
  113.1 8.3 %collective-permute-done.10.refs_4_ = bf16[224,1024]{1,0:T(8,128)(2,1)S(1)} collective-permute-done((bf16[224,1024]{1,0:T(8,128)(2,1)S(1)}, bf16[224,1024]{1,0:T(8,128)(2,1)S(1)}, u32[]{:S(2)}, u32[]{:S(2)}) %collective-permute-start.10) | collective-permute-done | bytes 458784 | tf_op jit(solution)/shard_map/ppermute | solution.py:254
  123.5 6.5 %collective-permute-done.28.refs_15_ = bf16[224,896]{1,0:T(8,128)(2,1)S(1)} collective-permute-done((bf16[224,896]{1,0:T(8,128)(2,1)S(1)}, bf16[224,896]{1,0:T(8,128)(2,1)S(1)}, u32[]{:S(2)}, u32[]{:S(2)}) %collective-permute-start.28) | collective-permute-done | bytes 401440 | tf_op jit(solution)/shard_map/ppermute | solution.py:254
  135.2 4.6 %collective-permute-done.12.refs_6_ = bf16[224,1024]{1,0:T(8,128)(2,1)S(1)} collective-permute-done((bf16[224,1024]{1,0:T(8,128)(2,1)S(1)}, bf16[224,1024]{1,0:T(8,128)(2,1)S(1)}, u32[]{:S(2)}, u32[]{:S(2)}) %collective-permute-start.12) | collective-permute-done | bytes 458784 | tf_op jit(solution)/shard_map/ppermute | solution.py:254
  140.3 3.1 %collective-permute-done.11.refs_5_ = bf16[224,1024]{1,0:T(8,128)(2,1)} collective-permute-done((bf16[224,1024]{1,0:T(8,128)(2,1)S(1)}, bf16[224,1024]{1,0:T(8,128)(2,1)}, u32[]{:S(2)}, u32[]{:S(2)}) %collective-permute-start.11) | collective-permute-done | bytes 458784 | tf_op jit(solution)/shard_map/ppermute | solution.py:254
  144.8 3.1 %collective-permute-done.30.refs_17_ = bf16[224,896]{1,0:T(8,128)(2,1)S(1)} collective-permute-done((bf16[224,896]{1,0:T(8,128)(2,1)S(1)}, bf16[224,896]{1,0:T(8,128)(2,1)S(1)}, u32[]{:S(2)}, u32[]{:S(2)}) %collective-permute-start.30) | collective-permute-done | bytes 401440 | tf_op jit(solution)/shard_map/ppermute | solution.py:254
  149.4 2.6 %collective-permute-done.29.refs_16_ = bf16[224,896]{1,0:T(8,128)(2,1)S(1)} collective-permute-done((bf16[224,896]{1,0:T(8,128)(2,1)S(1)}, bf16[224,896]{1,0:T(8,128)(2,1)S(1)}, u32[]{:S(2)}, u32[]{:S(2)}) %collective-permute-start.29) | collective-permute-done | bytes 401440 | tf_op jit(solution)/shard_map/ppermute | solution.py:254
  154.2 6.6 %collective-permute-done.32.refs_19_ = bf16[112,896]{1,0:T(8,128)(2,1)S(1)} collective-permute-done((bf16[112,896]{1,0:T(8,128)(2,1)S(1)}, bf16[112,896]{1,0:T(8,128)(2,1)S(1)}, u32[]{:S(2)}, u32[]{:S(2)}) %collective-permute-start.32) | collective-permute-done | bytes 200736 | tf_op jit(solution)/shard_map/ppermute | solution.py:254
  160.8 4.9 %collective-permute-done.31.refs_18_ = bf16[112,896]{1,0:T(8,128)(2,1)S(1)} collective-permute-done((bf16[112,896]{1,0:T(8,128)(2,1)S(1)}, bf16[112,896]{1,0:T(8,128)(2,1)S(1)}, u32[]{:S(2)}, u32[]{:S(2)}) %collective-permute-start.31) | collective-permute-done | bytes 200736 | tf_op jit(solution)/shard_map/ppermute | solution.py:254
  170.4 5.4 %collective-permute-done.16.refs_10_ = bf16[112,1024]{1,0:T(8,128)(2,1)} collective-permute-done((bf16[112,1024]{1,0:T(8,128)(2,1)S(1)}, bf16[112,1024]{1,0:T(8,128)(2,1)}, u32[]{:S(2)}, u32[]{:S(2)}) %collective-permute-start.16) | collective-permute-done | bytes 229408 | tf_op jit(solution)/shard_map/ppermute | solution.py:254
  178.8 41.4 %shard_map.30 = (bf16[512,1792]{1,0:T(8,128)(2,1)}, bf16[512,1792]{1,0:T(8,128)(2,1)}) custom-call(s32[19]{0:T(128)} %stack.49.place_ref, bf16[1024,1792]{1,0:T(8,128)(2,1)} %refs_0_.1, bf16[1024,1792]{1,0:T(8,128)(2,1)} %collective-permute-done.other_ref.refs_1_, bf16[224,1024]{1,0:T(8,128)(2,1)} %copy-done.3, bf16[224,1024]{1,0:T(8,128)(2,1)} %copy-done.11, ...), custom_call_target="tpu_custom_call" | custom-call | flops 26306674688 | bytes 25690112 | tf_op jit(solution)/shard_map/pallas_call | solution.py:167
  220.5 3.9 %collective-permute-done.51.got_ref = bf16[512,1792]{1,0:T(8,128)(2,1)S(1)} collective-permute-done((bf16[512,1792]{1,0:T(8,128)(2,1)}, bf16[512,1792]{1,0:T(8,128)(2,1)S(1)}, u32[]{:S(2)}, u32[]{:S(2)}) %collective-permute-start.51) | collective-permute-done | bytes 1835040 | tf_op jit(solution)/shard_map/ppermute | solution.py:287
  225.6 4.1 %shard_map.31 = bf16[1024,1792]{1,0:T(8,128)(2,1)} custom-call(s32[1]{0:T(128)} %bitcast.core_ref, bf16[512,1792]{1,0:T(8,128)(2,1)} %get-tuple-element.11.keep_ref, bf16[512,1792]{1,0:T(8,128)(2,1)} %copy-done.2), custom_call_target="tpu_custom_call" | custom-call | tf_op jit(solution)/shard_map/pallas_call | solution.py:197
  (168 shorter events, 70.4 us)
Async XLA Ops:
  34.5 18.8 %collective-permute-start.2 = (bf16[224,1024]{1,0:T(8,128)(2,1)S(1)}, bf16[224,1024]{1,0:T(8,128)(2,1)S(1)}, u32[]{:S(2)}, u32[]{:S(2)}) collective-permute-start(bf16[224,1024]{1,0:T(8,128)(2,1)S(1)} %pad_maximum_fusion), channel_id=1, source_target_pairs={{0,4},{4,8},{8,12},{12,14},{14,10},{10,6},{6,2},{2,0},{1,5},{5,9},... | collective-permute-start | bytes 1376264 | tf_op jit(solution)/shard_map/ppermute | solution.py:232
  37.0 21.3 %collective-permute-start.22 = (bf16[224,896]{1,0:T(8,128)(2,1)}, bf16[224,896]{1,0:T(8,128)(2,1)}, u32[]{:S(2)}, u32[]{:S(2)}) collective-permute-start(bf16[224,896]{1,0:T(8,128)(2,1)} %pad_maximum_fusion.3), channel_id=1, source_target_pairs={{0,2},{4,0},{8,4},{12,8},{14,12},{10,14},{6,10},{2,6},{1,3},{5,1},... | collective-permute-start | bytes 1204232 | tf_op jit(solution)/shard_map/ppermute | solution.py:232
  38.2 26.1 %collective-permute-start.6 = (bf16[224,1024]{1,0:T(8,128)(2,1)}, bf16[224,1024]{1,0:T(8,128)(2,1)}, u32[]{:S(2)}, u32[]{:S(2)}) collective-permute-start(bf16[224,1024]{1,0:T(8,128)(2,1)} %pad_maximum_fusion.1), channel_id=1, source_target_pairs={{0,2},{4,0},{8,4},{12,8},{14,12},{10,14},{6,10},{2,6},{1,3},{5,1},... | collective-permute-start | bytes 1376264 | tf_op jit(solution)/shard_map/ppermute | solution.py:232
  44.4 17.7 %collective-permute-start.19 = (bf16[224,896]{1,0:T(8,128)(2,1)}, bf16[224,896]{1,0:T(8,128)(2,1)}, u32[]{:S(2)}, u32[]{:S(2)}) collective-permute-start(bf16[224,896]{1,0:T(8,128)(2,1)} %add_convert_fusion.9), channel_id=1, source_target_pairs={{0,4},{4,8},{8,12},{12,14},{14,10},{10,6},{6,2},{2,0},{1,5},{5,9},... | collective-permute-start | bytes 1204232 | tf_op jit(solution)/shard_map/ppermute | solution.py:232
  55.4 14.2 %collective-permute-start.3 = (bf16[224,1024]{1,0:T(8,128)(2,1)}, bf16[224,1024]{1,0:T(8,128)(2,1)}, u32[]{:S(2)}, u32[]{:S(2)}) collective-permute-start(bf16[224,1024]{1,0:T(8,128)(2,1)} %add_convert_fusion.4), channel_id=1, source_target_pairs={{0,4},{4,8},{8,12},{12,14},{14,10},{10,6},{6,2},{2,0},{1,5},{5,9},... | collective-permute-start | bytes 1376264 | tf_op jit(solution)/shard_map/ppermute | solution.py:232
  72.3 13.8 %collective-permute-start.7 = (bf16[224,1024]{1,0:T(8,128)(2,1)}, bf16[224,1024]{1,0:T(8,128)(2,1)}, u32[]{:S(2)}, u32[]{:S(2)}) collective-permute-start(bf16[224,1024]{1,0:T(8,128)(2,1)} %get-tuple-element.14), channel_id=1, source_target_pairs={{0,2},{4,0},{8,4},{12,8},{14,12},{10,14},{6,10},{2,6},{1,3},{5,1},... | collective-permute-start | bytes 1376264 | tf_op jit(solution)/shard_map/ppermute | solution.py:232
  73.8 15.9 %collective-permute-start.20 = (bf16[224,896]{1,0:T(8,128)(2,1)}, bf16[224,896]{1,0:T(8,128)(2,1)}, u32[]{:S(2)}, u32[]{:S(2)}) collective-permute-start(bf16[224,896]{1,0:T(8,128)(2,1)} %get-tuple-element.21), channel_id=1, source_target_pairs={{0,4},{4,8},{8,12},{12,14},{14,10},{10,6},{6,2},{2,0},{1,5},{5,9},... | collective-permute-start | bytes 1204232 | tf_op jit(solution)/shard_map/ppermute | solution.py:232
  76.9 17.8 %collective-permute-start.24 = (bf16[224,896]{1,0:T(8,128)(2,1)}, bf16[224,896]{1,0:T(8,128)(2,1)}, u32[]{:S(2)}, u32[]{:S(2)}) collective-permute-start(bf16[224,896]{1,0:T(8,128)(2,1)} %add_convert_fusion.6), channel_id=1, source_target_pairs={{0,2},{4,0},{8,4},{12,8},{14,12},{10,14},{6,10},{2,6},{1,3},{5,1},... | collective-permute-start | bytes 1204232 | tf_op jit(solution)/shard_map/ppermute | solution.py:232
  77.7 20.4 %collective-permute-start.4 = (bf16[224,1024]{1,0:T(8,128)(2,1)}, bf16[224,1024]{1,0:T(8,128)(2,1)}, u32[]{:S(2)}, u32[]{:S(2)}) collective-permute-start(bf16[224,1024]{1,0:T(8,128)(2,1)} %get-tuple-element.13), channel_id=1, source_target_pairs={{0,4},{4,8},{8,12},{12,14},{14,10},{10,6},{6,2},{2,0},{1,5},{5,9},... | collective-permute-start | bytes 1376264 | tf_op jit(solution)/shard_map/ppermute | solution.py:232
  88.2 15.0 %collective-permute-start.8 = (bf16[224,1024]{1,0:T(8,128)(2,1)}, bf16[224,1024]{1,0:T(8,128)(2,1)}, u32[]{:S(2)}, u32[]{:S(2)}) collective-permute-start(bf16[224,1024]{1,0:T(8,128)(2,1)} %add_convert_fusion.1), channel_id=1, source_target_pairs={{0,2},{4,0},{8,4},{12,8},{14,12},{10,14},{6,10},{2,6},{1,3},{5,1},... | collective-permute-start | bytes 1376264 | tf_op jit(solution)/shard_map/ppermute | solution.py:232
  96.1 15.5 %collective-permute-start.26 = (bf16[224,896]{1,0:T(8,128)(2,1)S(1)}, bf16[224,896]{1,0:T(8,128)(2,1)S(1)}, u32[]{:S(2)}, u32[]{:S(2)}) collective-permute-start(bf16[224,896]{1,0:T(8,128)(2,1)S(1)} %add_convert_fusion.5.refs_11_), channel_id=1, source_target_pairs={{0,2},{4,0},{8,4},{12,8},{14,12},{10,14},{6,10},{2,6},{1,3},{5,1},... | collective-permute-start | bytes 1204232 | tf_op jit(solution)/shard_map/ppermute | solution.py:254
  97.0 14.6 %collective-permute-start.25 = (bf16[224,896]{1,0:T(8,128)(2,1)S(1)}, bf16[224,896]{1,0:T(8,128)(2,1)S(1)}, u32[]{:S(2)}, u32[]{:S(2)}) collective-permute-start(bf16[224,896]{1,0:T(8,128)(2,1)S(1)} %add_convert_fusion.5.refs_11_), channel_id=1, source_target_pairs={{0,4},{4,8},{8,12},{12,14},{14,10},{10,6},{6,2},{2,0},{1,5},{5,9},... | collective-permute-start | bytes 1204232 | tf_op jit(solution)/shard_map/ppermute | solution.py:254
  104.9 16.5 %collective-permute-start.10 = (bf16[224,1024]{1,0:T(8,128)(2,1)S(1)}, bf16[224,1024]{1,0:T(8,128)(2,1)S(1)}, u32[]{:S(2)}, u32[]{:S(2)}) collective-permute-start(bf16[224,1024]{1,0:T(8,128)(2,1)S(1)} %add_convert_fusion.refs_2_), channel_id=1, source_target_pairs={{0,2},{4,0},{8,4},{12,8},{14,12},{10,14},{6,10},{2,6},{1,3},{5,1},... | collective-permute-start | bytes 1376264 | tf_op jit(solution)/shard_map/ppermute | solution.py:254
  107.1 14.3 %collective-permute-start.9 = (bf16[224,1024]{1,0:T(8,128)(2,1)S(1)}, bf16[224,1024]{1,0:T(8,128)(2,1)S(1)}, u32[]{:S(2)}, u32[]{:S(2)}) collective-permute-start(bf16[224,1024]{1,0:T(8,128)(2,1)S(1)} %add_convert_fusion.refs_2_), channel_id=1, source_target_pairs={{0,4},{4,8},{8,12},{12,14},{14,10},{10,6},{6,2},{2,0},{1,5},{5,9},... | collective-permute-start | bytes 1376264 | tf_op jit(solution)/shard_map/ppermute | solution.py:254
  111.6 18.4 %collective-permute-start.28 = (bf16[224,896]{1,0:T(8,128)(2,1)S(1)}, bf16[224,896]{1,0:T(8,128)(2,1)S(1)}, u32[]{:S(2)}, u32[]{:S(2)}) collective-permute-start(bf16[224,896]{1,0:T(8,128)(2,1)S(1)} %collective-permute-done.26.refs_13_), channel_id=1, source_target_pairs={{0,2},{4,0},{8,4},{12,8},{14,12},{10,14},{6,10},{2,6},{1,3},{5,1},... | collective-permute-start | bytes 1204232 | tf_op jit(solution)/shard_map/ppermute | solution.py:254
  113.0 17.0 %collective-permute-start.43 = (bf16[224,896]{1,0:T(8,128)(2,1)S(1)}, bf16[224,896]{1,0:T(8,128)(2,1)S(1)}, u32[]{:S(2)}, u32[]{:S(2)}) collective-permute-start(bf16[224,896]{1,0:T(8,128)(2,1)S(1)} %collective-permute-done.25.refs_12_), channel_id=1, source_target_pairs={{0,1},{1,0},{2,3},{3,2},{4,5},{5,4},{6,7},{7,6},{8,9},{9,8},{10,11... | collective-permute-start | bytes 1204232 | tf_op jit(solution)/shard_map/ppermute | solution.py:285
  123.0 16.8 %collective-permute-start.12 = (bf16[224,1024]{1,0:T(8,128)(2,1)S(1)}, bf16[224,1024]{1,0:T(8,128)(2,1)S(1)}, u32[]{:S(2)}, u32[]{:S(2)}) collective-permute-start(bf16[224,1024]{1,0:T(8,128)(2,1)S(1)} %collective-permute-done.10.refs_4_), channel_id=1, source_target_pairs={{0,2},{4,0},{8,4},{12,8},{14,12},{10,14},{6,10},{2,6},{1,3},{5,1},... | collective-permute-start | bytes 1376264 | tf_op jit(solution)/shard_map/ppermute | solution.py:254
  133.1 14.8 %collective-permute-start.30 = (bf16[224,896]{1,0:T(8,128)(2,1)S(1)}, bf16[224,896]{1,0:T(8,128)(2,1)S(1)}, u32[]{:S(2)}, u32[]{:S(2)}) collective-permute-start(bf16[224,896]{1,0:T(8,128)(2,1)S(1)} %collective-permute-done.28.refs_15_), channel_id=1, source_target_pairs={{0,2},{4,0},{8,4},{12,8},{14,12},{10,14},{6,10},{2,6},{1,3},{5,1},... | collective-permute-start | bytes 1204232 | tf_op jit(solution)/shard_map/ppermute | solution.py:254
  134.5 17.5 %collective-permute-start.29 = (bf16[224,896]{1,0:T(8,128)(2,1)S(1)}, bf16[224,896]{1,0:T(8,128)(2,1)S(1)}, u32[]{:S(2)}, u32[]{:S(2)}) collective-permute-start(bf16[224,896]{1,0:T(8,128)(2,1)S(1)} %collective-permute-done.27.refs_14_), channel_id=1, source_target_pairs={{0,4},{4,8},{8,12},{12,14},{14,10},{10,6},{6,2},{2,0},{1,5},{5,9},... | collective-permute-start | bytes 1204232 | tf_op jit(solution)/shard_map/ppermute | solution.py:254
  139.8 13.5 %collective-permute-start.46 = (bf16[224,896]{1,0:T(8,128)(2,1)S(1)}, bf16[224,896]{1,0:T(8,128)(2,1)S(1)}, u32[]{:S(2)}, u32[]{:S(2)}) collective-permute-start(bf16[224,896]{1,0:T(8,128)(2,1)S(1)} %collective-permute-done.28.refs_15_), channel_id=1, source_target_pairs={{0,1},{1,0},{2,3},{3,2},{4,5},{5,4},{6,7},{7,6},{8,9},{9,8},{10,11... | collective-permute-start | bytes 1204232 | tf_op jit(solution)/shard_map/ppermute | solution.py:285
  139.8 14.3 %collective-permute-start.45 = (bf16[224,896]{1,0:T(8,128)(2,1)S(1)}, bf16[224,896]{1,0:T(8,128)(2,1)S(1)}, u32[]{:S(2)}, u32[]{:S(2)}) collective-permute-start(bf16[224,896]{1,0:T(8,128)(2,1)S(1)} %collective-permute-done.27.refs_14_), channel_id=1, source_target_pairs={{0,1},{1,0},{2,3},{3,2},{4,5},{5,4},{6,7},{7,6},{8,9},{9,8},{10,11... | collective-permute-start | bytes 1204232 | tf_op jit(solution)/shard_map/ppermute | solution.py:285
  143.5 22.2 %collective-permute-start.14 = (bf16[224,1024]{1,0:T(8,128)(2,1)S(1)}, bf16[224,1024]{1,0:T(8,128)(2,1)S(1)}, u32[]{:S(2)}, u32[]{:S(2)}) collective-permute-start(bf16[224,1024]{1,0:T(8,128)(2,1)S(1)} %collective-permute-done.12.refs_6_), channel_id=1, source_target_pairs={{0,2},{4,0},{8,4},{12,8},{14,12},{10,14},{6,10},{2,6},{1,3},{5,1},... | collective-permute-start | bytes 1376264 | tf_op jit(solution)/shard_map/ppermute | solution.py:254
  147.9 18.3 %collective-permute-start.13 = (bf16[224,1024]{1,0:T(8,128)(2,1)}, bf16[224,1024]{1,0:T(8,128)(2,1)S(1)}, u32[]{:S(2)}, u32[]{:S(2)}) collective-permute-start(bf16[224,1024]{1,0:T(8,128)(2,1)} %collective-permute-done.11.refs_5_), channel_id=1, source_target_pairs={{0,4},{4,8},{8,12},{12,14},{14,10},{10,6},{6,2},{2,0},{1,5},{5,9},... | collective-permute-start | bytes 1376264 | tf_op jit(solution)/shard_map/ppermute | solution.py:254
  154.1 15.8 %collective-permute-start.37 = (bf16[224,1024]{1,0:T(8,128)(2,1)S(1)}, bf16[224,1024]{1,0:T(8,128)(2,1)S(1)}, u32[]{:S(2)}, u32[]{:S(2)}) collective-permute-start(bf16[224,1024]{1,0:T(8,128)(2,1)S(1)} %collective-permute-done.12.refs_6_), channel_id=1, source_target_pairs={{0,1},{1,0},{2,3},{3,2},{4,5},{5,4},{6,7},{7,6},{8,9},{9,8},{10,11... | collective-permute-start | bytes 1376264 | tf_op jit(solution)/shard_map/ppermute | solution.py:285
  (59 other events, 915.8 us)

commit v3 on v2

v3 whole, which is shorter than its diff:
```python
import functools

import jax
import jax.numpy as jnp
from jax import lax
from jax.experimental import pallas as pl
from jax.experimental.pallas import tpu as pltpu
from jax.sharding import PartitionSpec as P

R = 8192

coef_linear = 3.4445
coef_cubic = -4.775
coef_quintic = 2.0315

PANEL = 256
RING_MOST = 16
STEP_BYTES = 20 * 2**20
STEP_FLOPS = 8 * 10**9
F32 = jnp.float32
BF16 = jnp.bfloat16


def dot(a, b, ca, cb):
    return lax.dot_general(a, b, (((ca,), (cb,)), ((), ())), preferred_element_type=F32)


def diag_kernel(x_ref, o_ref, wide):
    half = x_ref.shape[1]
    width = o_ref.shape[1]
    wide[:, :half] = x_ref[...]
    wide[:, half:] = x_ref[:, : width - PANEL]
    for at in range(0, half, PANEL):
        strip = dot(x_ref[:, at : at + PANEL], wide[:, at : at + width], 0, 0)
        o_ref[at : at + PANEL, :] = (strip * (1.0 / R)).astype(BF16)


def diag_gram(x, width):
    rows, half = x.shape
    vmem = pl.BlockSpec(memory_space=pltpu.VMEM)
    return pl.pallas_call(
        diag_kernel,
        out_shape=jax.ShapeDtypeStruct((half, width), BF16),
        in_specs=[vmem],
        out_specs=vmem,
        scratch_shapes=[pltpu.VMEM((rows, half + width - PANEL), BF16)],
        compiler_params=pltpu.CompilerParams(vmem_limit_bytes=40 * 2**20),
        cost_estimate=pl.CostEstimate(flops=2 * rows * half * width, bytes_accessed=4 * rows * half, transcendentals=0),
    )(x)


def side_kernel(core_ref, own_ref, other_ref, o_ref):
    half = own_ref.shape[1]
    part = half // 2

    def go(left_ref, right_ref, start):
        for at in range(0, half, PANEL):
            strip = dot(left_ref[:, at : at + PANEL], right_ref[:, start : start + part], 0, 0)
            o_ref[at : at + PANEL, :] = (strip * (1.0 / R)).astype(BF16)

    @pl.when(core_ref[0] == 0)
    def _():
        go(own_ref, other_ref, 0)

    @pl.when(core_ref[0] == 1)
    def _():
        go(other_ref, own_ref, part)


def side_gram(core, own, other):
    rows, half = own.shape
    vmem = pl.BlockSpec(memory_space=pltpu.VMEM)
    return pl.pallas_call(
        side_kernel,
        out_shape=jax.ShapeDtypeStruct((half, half // 2), BF16),
        in_specs=[pl.BlockSpec(memory_space=pltpu.SMEM), vmem, vmem],
        out_specs=vmem,
        compiler_params=pltpu.CompilerParams(vmem_limit_bytes=40 * 2**20),
        cost_estimate=pl.CostEstimate(flops=STEP_FLOPS, bytes_accessed=6 * rows * half, transcendentals=0),
    )(core.reshape(1), own, other)


def finish_kernel(panels, reach, part, pieces, place_ref, *refs):
    own_ref, other_ref = refs[:2]
    piece_refs = refs[2 : 2 + 2 * sum(pieces)]
    keep_ref, send_ref, xe, ye, yf, diag, side, out, sems = refs[2 + 2 * sum(pieces) :]
    core = place_ref[0]
    rows = xe.shape[1]
    half = panels * PANEL
    width = reach * PANEL

    copies = []

    def bring(source, target):
        copy = pltpu.make_async_copy(source, target, sems.at[len(copies)])
        copy.start()
        copies.append(copy)

    mine = pl.ds(pl.multiple_of(core * rows, rows), rows)
    bring(own_ref.at[mine, :], xe.at[core, :, pl.ds(0, half)])
    bring(other_ref.at[mine, :], xe.at[1 - core, :, pl.ds(0, half)])
    at = 0
    for owner in (core, 1 - core):
        for k, store in enumerate((diag, side)):
            for m in range(pieces[k]):
                piece = piece_refs[at]
                start = place_ref[1 + m + (pieces[0] if k == 1 else 0)]
                start = pl.multiple_of(start, 16)
                bring(piece, store.at[owner, pl.ds(start, piece.shape[0]), :])
                at += 1
    early = 2 + pieces[0]
    late = early + pieces[1]
    diag_copies = copies[:early] + copies[late : late + pieces[0]]
    side_copies = copies[early:late] + copies[late + pieces[0] :]

    def around(src, h, j):
        at = pl.multiple_of(j * PANEL, PANEL)
        total = dot(src[h, :, pl.ds(at, width)], diag[h, pl.ds(at, PANEL), :], 1, 1)
        for d in range(1, reach):
            there = pl.ds(pl.multiple_of(lax.rem(j + panels - d, panels) * PANEL, PANEL), PANEL)
            total += dot(src[h, :, there], diag[h, there, d * PANEL : (d + 1) * PANEL], 1, 0)
        return total

    def across(src, h, b):
        if h == 1:
            return dot(src[0, :, :half], side[b], 1, 0)
        here = slice(b * part, (b + 1) * part)
        return sum(dot(src[1, :, e * part : (e + 1) * part], side[e, here, :], 1, 1) for e in range(2))

    for copy in diag_copies:
        copy.wait()
    for h in range(2):
        xe[h, :, half:] = xe[h, :, : width - PANEL]

    @pl.loop(0, panels)
    def _(j):
        here = pl.ds(pl.multiple_of(j * PANEL, PANEL), PANEL)
        for h in range(2):
            yf[h, :, here] = around(xe, h, j)

    for copy in side_copies:
        copy.wait()
    for h in range(2):
        for b in range(2):
            here = slice(b * part, (b + 1) * part)
            total = yf[h, :, here] + across(xe, h, b)
            ye[h, :, here] = total.astype(BF16)
            yf[h, :, here] = coef_linear * xe[h, :, here].astype(F32) + coef_cubic * total
    for h in range(2):
        ye[h, :, half:] = ye[h, :, : width - PANEL]

    for h in range(2):
        for b in range(2):
            here = slice(b * part, (b + 1) * part)
            yf[h, :, here] += coef_quintic * across(ye, h, b)

    @pl.loop(0, panels)
    def _(j):
        here = pl.ds(pl.multiple_of(j * PANEL, PANEL), PANEL)
        for h in range(2):
            out[h, :, here] = (yf[h, :, here] + coef_quintic * around(ye, h, j)).astype(BF16)

    last = [
        pltpu.make_async_copy(out.at[core], keep_ref.at[mine, :], sems.at[0]),
        pltpu.make_async_copy(out.at[1 - core], send_ref, sems.at[1]),
    ]
    for copy in last:
        copy.start()
    for copy in last:
        copy.wait()


def finish(core, own, other, starts, mine, theirs, panels, reach):
    rows, half = own.shape
    share = rows // 2
    part = half // 2
    width = reach * PANEL
    pieces = tuple(len(p) for p in mine)
    operands = [own, other, *mine[0], *mine[1], *theirs[0], *theirs[1]]
    place = jnp.stack([core, *starts]).astype(jnp.int32)
    anywhere = pl.BlockSpec(memory_space=pl.ANY)
    return pl.pallas_call(
        functools.partial(finish_kernel, panels, reach, part, pieces),
        out_shape=[jax.ShapeDtypeStruct((n, half), BF16) for n in (rows, share)],
        in_specs=[pl.BlockSpec(memory_space=pltpu.SMEM)] + [anywhere] * len(operands),
        out_specs=[anywhere] * 2,
        scratch_shapes=[
            pltpu.VMEM((2, share, half + width - PANEL), BF16),
            pltpu.VMEM((2, share, half + width - PANEL), BF16),
            pltpu.VMEM((2, share, half), F32),
            pltpu.VMEM((2, half, width), BF16),
            pltpu.VMEM((2, half, part), BF16),
            pltpu.VMEM((2, share, half), BF16),
            pltpu.SemaphoreType.DMA((len(operands),)),
        ],
        compiler_params=pltpu.CompilerParams(vmem_limit_bytes=56 * 2**20),
        cost_estimate=pl.CostEstimate(flops=16 * share * half * half, bytes_accessed=8 * half * half, transcendentals=0),
    )(place, *operands)


def add_kernel(kind, place_ref, forth_ref, back_ref, block_ref, *refs):
    out_refs, (own, sems) = refs[-4:-2] if kind != "last" else refs[-3:-2], refs[-2:]
    size = out_refs[0].shape[0]
    middle = size // 2
    copies = []
    for i in range(len(out_refs)):
        start = pl.multiple_of(place_ref[i], 16)
        copies.append(pltpu.make_async_copy(block_ref.at[pl.ds(start, size), :], own.at[i], sems.at[i]))
    for copy in copies:
        copy.start()
    for copy in copies:
        copy.wait()

    if kind == "last":
        total = own[0].astype(F32) + forth_ref[...].astype(F32) + back_ref[...].astype(F32)
        out_refs[0][...] = total.astype(BF16)
    elif kind == "middle":
        out_refs[0][...] = own[0] + forth_ref[...]
        out_refs[1][...] = own[1] + back_ref[...]
    else:
        out_refs[0][:middle] = own[0, :middle] + forth_ref[...]
        out_refs[0][middle:] = own[0, middle:]
        out_refs[1][:middle] = own[1, :middle]
        out_refs[1][middle:] = own[1, middle:] + back_ref[...]


def add_step(kind, size, starts, forth, back, block, after):
    outs = 1 if kind == "last" else 2
    cols = block.shape[1]
    vmem = pl.BlockSpec(memory_space=pltpu.VMEM)
    anywhere = pl.BlockSpec(memory_space=pl.ANY)
    return pl.pallas_call(
        functools.partial(add_kernel, kind),
        out_shape=[jax.ShapeDtypeStruct((size, cols), BF16)] * outs,
        in_specs=[pl.BlockSpec(memory_space=pltpu.SMEM), vmem, vmem] + [anywhere] * (1 + len(after)),
        out_specs=[vmem] * outs,
        scratch_shapes=[pltpu.VMEM((outs, size, cols), BF16), pltpu.SemaphoreType.DMA((outs,))],
        cost_estimate=pl.CostEstimate(flops=STEP_FLOPS // 2, bytes_accessed=8 * size * cols, transcendentals=0),
    )(jnp.stack(starts).astype(jnp.int32), forth, back, block, *after)


def gate(values, after):
    anywhere = pl.BlockSpec(memory_space=pl.ANY)
    return pl.pallas_call(
        lambda *refs: None,
        out_shape=[jax.ShapeDtypeStruct(v.shape, v.dtype) for v in values],
        in_specs=[anywhere] * (len(values) + len(after)),
        out_specs=[anywhere] * len(values),
        input_output_aliases={i: i for i in range(len(values))},
        cost_estimate=pl.CostEstimate(flops=STEP_FLOPS, bytes_accessed=STEP_BYTES, transcendentals=0),
    )(*values, *after)


def ring_exchange(blocks):
    count = lax.axis_size("row")
    order = list(range(0, count, 2)) + list(range(1, count, 2))[::-1]
    places = [order.index(r) for r in range(count)]
    place = jnp.array(places, jnp.int32)[lax.axis_index("row")]
    far = count // 2
    turns = (1, -1)
    pairs = {t: [(order[p], order[(p + t) % count]) for p in range(count)] for t in turns}
    sizes = [b.shape[0] // count for b in blocks]
    parts = range(len(blocks))

    def row_of(k, distance):
        return lax.rem(place + distance + count, count) * sizes[k]

    def half_of(value, turn):
        middle = value.shape[0] // 2
        return value[:middle] if turn == 1 else value[middle:]

    def pass_on(values):
        return [lax.ppermute(v, "row", pairs[t]) for t, v in zip(turns, values, strict=True)]

    held = []
    for k in parts:
        whole = lax.dynamic_slice_in_dim(blocks[k], row_of(k, far), sizes[k], 0)
        held.append([half_of(whole, t) for t in turns])
    after = blocks[1:]
    for distance in range(far - 1, -1, -1):
        kind = "last" if distance == 0 else "first" if distance == far - 1 else "middle"
        for k in parts:
            forth, back = pass_on(held[k])
            starts = [row_of(k, distance), row_of(k, -distance)][: 1 if distance == 0 else 2]
            held[k] = add_step(kind, sizes[k], starts, forth, back, blocks[k], after)
            after = [held[k][0]]
    pieces = [[held[k][0]] for k in parts]
    starts = [[row_of(k, 0)] for k in parts]
    held = [[h[0], h[0]] for h in held]
    for distance in range(1, far + 1):
        for k in parts:
            if distance == far:
                held[k] = [half_of(h, t) for t, h in zip(turns, held[k], strict=True)]
            held[k] = gate(pass_on(held[k]), after)
            after = [held[k][0]]
            pieces[k] += held[k]
            ends = [row_of(k, -distance), row_of(k, distance)]
            if distance == far:
                ends[1] = ends[1] + sizes[k] // 2
            starts[k] += ends
    return pieces, starts[0] + starts[1]


def plain_exchange(blocks):
    pieces = []
    for block in blocks:
        mine = lax.psum_scatter(block, "row", scatter_dimension=0, tiled=True)
        pieces.append([lax.all_gather(mine, "row", axis=0, tiled=True)])
    return pieces, [jnp.int32(0)] * len(blocks)


def body(iterate):
    half = iterate.shape[1]
    count = lax.axis_size("row")
    core = lax.axis_index("col")
    panels = half // PANEL
    reach = (panels + 1) // 2
    swap = [(0, 1), (1, 0)]

    other = lax.ppermute(iterate, "col", swap)
    diag_part = diag_gram(iterate, reach * PANEL)
    side_part = side_gram(core, iterate, other)
    exchange = ring_exchange if count <= RING_MOST else plain_exchange
    mine, starts = exchange([diag_part, side_part])
    theirs = [[lax.ppermute(piece, "col", swap) for piece in kind] for kind in mine]
    keep, send = finish(core, iterate, other, starts, mine, theirs, panels, reach)
    got = lax.ppermute(send, "col", swap)
    return lax.dynamic_update_slice_in_dim(keep, got, (1 - core) * got.shape[0], 0)


def solution(mesh):
    return jax.shard_map(
        body,
        mesh=mesh,
        in_specs=(P(("groups", "row"), "col"),),
        out_specs=P(("groups", "row"), "col"),
        check_vma=False,
    )
```

time: 230 us -> 218 us (0.948)
  waiting for transfers between devices: 101 us -> 74.5 us
  Pallas kernels: 55.6 us -> 76.3 us
  other arithmetic: 19.5 us -> 1.84 us
  local copies, waits for them, and re-layouts: 9.47 us -> 20.4 us
    ppermute x33, waiting for transfers between devices: 99.2 us -> 73.2 us  [the longest x32 69.6 us: pass_on(): lax.ppermute(v, 'row', pairs[t])]
    pallas_call x1 -> x16, Pallas kernels: 4.13 us -> 25.8 us  [the longest x8 25.8 us: add_step(): pl.pallas_call(functools.partial(add_kernel, kind), out_shape=[jax.ShapeD...]
    convert_element_type x10 -> x0, other arithmetic: 16.9 us -> none  [the longest x8 14.1 us: add(): return (a.astype(F32) + b.astype(F32)).astype(BF16)]
    unnamed x62 -> x82, local copies, waits for them, and re-layouts: 5.2 us -> 11.7 us
    slice x6, local copies, waits for them, and re-layouts: 2.29 us -> 5.41 us  [half_of(): return value[:middle] if turn == 1 else value[middle:]]
    concatenate x4 -> x0, other arithmetic: 2.58 us -> none  [the longest x2 1.59 us: ring_exchange(): jnp.concatenate([mine[:middle].astype(BF16), add(mine[middle:], arrived[t...]
  transfers between devices with their start and end apart: 52 -> 52, of which waited for: 25 -> 24; matrix products, arithmetic and copies ran while one was open for 10% -> 4% of each run, Pallas kernels for 2% -> 16%
where the time goes in v3:
time: 218 us
  Pallas kernels  76.3 us (35%)
  waiting for transfers between devices  74.5 us (34%)
  starting transfers between devices  38.4 us (18%)
  local copies, waits for them, and re-layouts  20.4 us (9%)
  between operations  6.12 us (3%)
    ppermute x32, waiting for transfers between devices, pass_on(): lax.ppermute(v, 'row', pairs[t])  69.6 us
    pallas_call x1, Pallas kernels, finish(): pl.pallas_call(functools.partial(finish_kernel, panels, reach, part, piec...  40.5 us
    ppermute x32, starting transfers between devices, pass_on(): lax.ppermute(v, 'row', pairs[t])  33.9 us
    pallas_call x8, Pallas kernels, add_step(): pl.pallas_call(functools.partial(add_kernel, kind), out_shape=[jax.ShapeD...  25.8 us
    unnamed x82, local copies, waits for them, and re-layouts  11.7 us
    pallas_call x1, Pallas kernels, side_gram(): pl.pallas_call(side_kernel, out_shape=jax.ShapeDtypeStruct((half, half //...  6.04 us
    slice x6, local copies, waits for them, and re-layouts, half_of(): return value[:middle] if turn == 1 else value[middle:]  5.41 us
  transfers between devices with their start and end apart: 52, of which 24 were waited for; matrix products, arithmetic and copies ran while one was open for 4% of the time, Pallas kernels for 16%

profile of v3, /device:TPU:0, one launch (start us, length us, event | category | flops | bytes accessed | tf_op | source)
XLA Modules:
  0.0 217.5 jit_solution(704669560367279820)
XLA Ops:
  2.4 2.0 copy-done.2
  4.4 4.0 %shard_map.28.block_ref = bf16[1792,1024]{1,0:T(8,128)(2,1)S(1)} custom-call(bf16[1024,1792]{1,0:T(8,128)(2,1)S(1)} %copy-done.2), custom_call_target="tpu_custom_call" | custom-call | flops 3758096384 | bytes 7340032 | tf_op jit(solution)/shard_map/pallas_call | solution.py:41
  11.0 2.5 %collective-permute-start.2 = (bf16[112,1024]{1,0:T(8,128)(2,1)}, bf16[112,1024]{1,0:T(8,128)(2,1)}, u32[]{:S(2)}, u32[]{:S(2)}) collective-permute-start(bf16[112,1024]{1,0:T(8,128)(2,1)} %get-tuple-element.65), channel_id=1, source_target_pairs={{0,2},{4,0},{8,4},{12,8},{14,12},{10,14},{6,10},{2,6},{1,3},{5,1},... | collective-permute-start | bytes 688136 | tf_op jit(solution)/shard_map/ppermute | solution.py:273
  17.9 2.0 copy-done.3
  20.0 6.0 %shard_map.29.refs_0_.block_ref = bf16[1792,896]{1,0:T(8,128)(2,1)S(1)} custom-call(s32[1]{0:T(128)} %bitcast.core_ref, bf16[1024,1792]{1,0:T(8,128)(2,1)S(1)} %copy-done.3, bf16[1024,1792]{1,0:T(8,128)(2,1)} %collective-permute-done.other_ref.refs_1_), custom_call_target="tpu_custom_call" | custom-call | flops 8000000000 | bytes 11010048 | tf_op jit(solution)/shard_map/pallas_call | solution.py:73
  29.0 3.3 %shard_map.30 = (bf16[224,1024]{1,0:T(8,128)(2,1)}, bf16[224,1024]{1,0:T(8,128)(2,1)}) custom-call(s32[2]{0:T(128)} %pad_add_fusion.2.place_ref, bf16[112,1024]{1,0:T(8,128)(2,1)} %collective-permute-done.1.forth_ref, bf16[112,1024]{1,0:T(8,128)(2,1)} %collective-permute-done.2.back_ref, bf16[1792,1024]{1,0:T(8,128)(2,1)} %copy-done, bf16[1792,896]{1,0:T(8,128)(2,1)} %copy-done.1), custom_call_target="tpu_custom_call" | custom-call | flops 4000000000 | bytes 1835008 | tf_op jit(solution)/shard_map/pallas_call | solution.py:232
  35.7 3.1 %shard_map.31 = (bf16[224,896]{1,0:T(8,128)(2,1)}, bf16[224,896]{1,0:T(8,128)(2,1)}) custom-call(s32[2]{0:T(128)} %pad_add_fusion.2.place_ref, bf16[112,896]{1,0:T(8,128)(2,1)} %collective-permute-done.5.forth_ref, bf16[112,896]{1,0:T(8,128)(2,1)} %collective-permute-done.6.back_ref, bf16[1792,896]{1,0:T(8,128)(2,1)} %copy-done.1, ...), custom_call_target="tpu_custom_call" | custom-call | flops 4000000000 | bytes 1605632 | tf_op jit(solution)/shard_map/pallas_call | solution.py:232
  40.9 5.0 %collective-permute-done.4.back_ref = bf16[224,1024]{1,0:T(8,128)(2,1)S(1)} collective-permute-done((bf16[224,1024]{1,0:T(8,128)(2,1)}, bf16[224,1024]{1,0:T(8,128)(2,1)S(1)}, u32[]{:S(2)}, u32[]{:S(2)}) %collective-permute-start.4) | collective-permute-done | bytes 458784 | tf_op jit(solution)/shard_map/ppermute | solution.py:273
  48.7 3.4 %shard_map.32 = (bf16[224,1024]{1,0:T(8,128)(2,1)}, bf16[224,1024]{1,0:T(8,128)(2,1)}) custom-call(s32[2]{0:T(128)} %pad_add_fusion.1.place_ref, bf16[224,1024]{1,0:T(8,128)(2,1)} %copy-done.24, bf16[224,1024]{1,0:T(8,128)(2,1)} %copy-done.21, bf16[1792,1024]{1,0:T(8,128)(2,1)} %copy-done, bf16[224,896]{1,0:T(8,128)(2,1)} %get-tuple-element.37.refs_0_), custom_call_target="tpu_custom_call" | custom-call | flops 4000000000 | bytes 1835008 | tf_op jit(solution)/shard_map/pallas_call | solution.py:232
  57.3 3.2 %shard_map.33 = (bf16[224,896]{1,0:T(8,128)(2,1)}, bf16[224,896]{1,0:T(8,128)(2,1)}) custom-call(s32[2]{0:T(128)} %pad_add_fusion.1.place_ref, bf16[224,896]{1,0:T(8,128)(2,1)} %copy-done.32, bf16[224,896]{1,0:T(8,128)(2,1)} %copy-done.30, bf16[1792,896]{1,0:T(8,128)(2,1)} %copy-done.1, bf16[224,1024]{1,0:T(8,128)(2,1)} %get-tuple-element.38.refs_0_), custom_call_target="tpu_custom_call" | custom-call | flops 4000000000 | bytes 1605632 | tf_op jit(solution)/shard_map/pallas_call | solution.py:232
  62.6 3.2 %collective-permute-done.8.back_ref = bf16[224,1024]{1,0:T(8,128)(2,1)S(1)} collective-permute-done((bf16[224,1024]{1,0:T(8,128)(2,1)}, bf16[224,1024]{1,0:T(8,128)(2,1)S(1)}, u32[]{:S(2)}, u32[]{:S(2)}) %collective-permute-start.8) | collective-permute-done | bytes 458784 | tf_op jit(solution)/shard_map/ppermute | solution.py:273
  68.2 3.4 %shard_map.34 = (bf16[224,1024]{1,0:T(8,128)(2,1)}, bf16[224,1024]{1,0:T(8,128)(2,1)}) custom-call(s32[2]{0:T(128)} %pad_add_fusion.place_ref, bf16[224,1024]{1,0:T(8,128)(2,1)} %copy-done.25, bf16[224,1024]{1,0:T(8,128)(2,1)} %copy-done.22, bf16[1792,1024]{1,0:T(8,128)(2,1)} %copy-done, bf16[224,896]{1,0:T(8,128)(2,1)} %get-tuple-element.41.refs_0_), custom_call_target="tpu_custom_call" | custom-call | flops 4000000000 | bytes 1835008 | tf_op jit(solution)/shard_map/pallas_call | solution.py:232
  76.8 3.2 %shard_map.35 = (bf16[224,896]{1,0:T(8,128)(2,1)}, bf16[224,896]{1,0:T(8,128)(2,1)}) custom-call(s32[2]{0:T(128)} %pad_add_fusion.place_ref, bf16[224,896]{1,0:T(8,128)(2,1)} %copy-done.29, bf16[224,896]{1,0:T(8,128)(2,1)} %copy-done.28, bf16[1792,896]{1,0:T(8,128)(2,1)} %copy-done.1, bf16[224,1024]{1,0:T(8,128)(2,1)} %get-tuple-element.42.refs_0_), custom_call_target="tpu_custom_call" | custom-call | flops 4000000000 | bytes 1605632 | tf_op jit(solution)/shard_map/pallas_call | solution.py:232
  82.1 3.2 %collective-permute-done.12.back_ref = bf16[224,1024]{1,0:T(8,128)(2,1)S(1)} collective-permute-done((bf16[224,1024]{1,0:T(8,128)(2,1)}, bf16[224,1024]{1,0:T(8,128)(2,1)S(1)}, u32[]{:S(2)}, u32[]{:S(2)}) %collective-permute-start.12) | collective-permute-done | bytes 458784 | tf_op jit(solution)/shard_map/ppermute | solution.py:273
  87.6 3.2 %shard_map.36.refs_0_.refs_2_ = bf16[224,1024]{1,0:T(8,128)(2,1)} custom-call(s32[1]{0:T(128)} %bitcast.2.place_ref, bf16[224,1024]{1,0:T(8,128)(2,1)} %copy-done.18, bf16[224,1024]{1,0:T(8,128)(2,1)} %copy-done.17, bf16[1792,1024]{1,0:T(8,128)(2,1)} %copy-done, bf16[224,896]{1,0:T(8,128)(2,1)} %get-tuple-element.45.refs_0_), custom_call_target="tpu_custom_call" | custom-call | flops 4000000000 | bytes 1835008 | tf_op jit(solution)/shard_map/pallas_call | solution.py:232
  95.9 3.0 %shard_map.37.refs_2_.refs_11_ = bf16[224,896]{1,0:T(8,128)(2,1)} custom-call(s32[1]{0:T(128)} %bitcast.2.place_ref, bf16[224,896]{1,0:T(8,128)(2,1)} %copy-done.33, bf16[224,896]{1,0:T(8,128)(2,1)} %copy-done.31, bf16[1792,896]{1,0:T(8,128)(2,1)} %copy-done.1, bf16[224,1024]{1,0:T(8,128)(2,1)} %shard_map.36.refs_0_.refs_2_), custom_call_target="tpu_custom_call" | custom-call | flops 4000000000 | bytes 1605632 | tf_op jit(solution)/shard_map/pallas_call | solution.py:232
  103.0 8.4 %collective-permute-done.22.refs_1_ = bf16[224,896]{1,0:T(8,128)(2,1)S(1)} collective-permute-done((bf16[224,896]{1,0:T(8,128)(2,1)}, bf16[224,896]{1,0:T(8,128)(2,1)S(1)}, u32[]{:S(2)}, u32[]{:S(2)}) %collective-permute-start.22) | collective-permute-done | bytes 401440 | tf_op jit(solution)/shard_map/ppermute | solution.py:273
  112.1 8.6 %collective-permute-done.20.refs_1_ = bf16[224,1024]{1,0:T(8,128)(2,1)S(1)} collective-permute-done((bf16[224,1024]{1,0:T(8,128)(2,1)}, bf16[224,1024]{1,0:T(8,128)(2,1)S(1)}, u32[]{:S(2)}, u32[]{:S(2)}) %collective-permute-start.20) | collective-permute-done | bytes 458784 | tf_op jit(solution)/shard_map/ppermute | solution.py:273
  124.1 7.7 %collective-permute-done.26.refs_1_ = bf16[224,896]{1,0:T(8,128)(2,1)S(1)} collective-permute-done((bf16[224,896]{1,0:T(8,128)(2,1)}, bf16[224,896]{1,0:T(8,128)(2,1)S(1)}, u32[]{:S(2)}, u32[]{:S(2)}) %collective-permute-start.26) | collective-permute-done | bytes 401440 | tf_op jit(solution)/shard_map/ppermute | solution.py:273
  133.8 9.3 %collective-permute-done.24.refs_1_ = bf16[224,1024]{1,0:T(8,128)(2,1)S(1)} collective-permute-done((bf16[224,1024]{1,0:T(8,128)(2,1)}, bf16[224,1024]{1,0:T(8,128)(2,1)S(1)}, u32[]{:S(2)}, u32[]{:S(2)}) %collective-permute-start.24) | collective-permute-done | bytes 458784 | tf_op jit(solution)/shard_map/ppermute | solution.py:273
  147.9 4.5 %collective-permute-done.30.refs_1_ = bf16[224,896]{1,0:T(8,128)(2,1)S(1)} collective-permute-done((bf16[224,896]{1,0:T(8,128)(2,1)}, bf16[224,896]{1,0:T(8,128)(2,1)S(1)}, u32[]{:S(2)}, u32[]{:S(2)}) %collective-permute-start.30) | collective-permute-done | bytes 401440 | tf_op jit(solution)/shard_map/ppermute | solution.py:273
  163.0 3.3 %collective-permute-done.31.refs_0_ = bf16[112,896]{1,0:T(8,128)(2,1)} collective-permute-done((bf16[112,896]{1,0:T(8,128)(2,1)S(1)}, bf16[112,896]{1,0:T(8,128)(2,1)}, u32[]{:S(2)}, u32[]{:S(2)}) %collective-permute-start.31) | collective-permute-done | bytes 200736 | tf_op jit(solution)/shard_map/ppermute | solution.py:273
  171.6 40.5 %shard_map.46 = (bf16[1024,1792]{1,0:T(8,128)(2,1)}, bf16[512,1792]{1,0:T(8,128)(2,1)}) custom-call(s32[19]{0:T(128)} %stack.38.place_ref, bf16[1024,1792]{1,0:T(8,128)(2,1)} %refs_0_.1, bf16[1024,1792]{1,0:T(8,128)(2,1)} %collective-permute-done.other_ref.refs_1_, bf16[224,1024]{1,0:T(8,128)(2,1)} %shard_map.36.refs_0_.refs_2_, ...), custom_call_target="tpu_custom_call" | custom-call | flops 26306674688 | bytes 25690112 | tf_op jit(solution)/shard_map/pallas_call | solution.py:182
  212.5 3.6 %collective-permute-done.51 = bf16[512,1792]{1,0:T(8,128)(2,1)S(1)} collective-permute-done((bf16[512,1792]{1,0:T(8,128)(2,1)}, bf16[512,1792]{1,0:T(8,128)(2,1)S(1)}, u32[]{:S(2)}, u32[]{:S(2)}) %collective-permute-start.51) | collective-permute-done | bytes 1835040 | tf_op jit(solution)/shard_map/ppermute | solution.py:327
  (193 shorter events, 71.6 us)
Async XLA Ops:
  0.0 17.9 %collective-permute-start = (bf16[1024,1792]{1,0:T(8,128)(2,1)}, bf16[1024,1792]{1,0:T(8,128)(2,1)}, u32[]{:S(2)}, u32[]{:S(2)}) collective-permute-start(bf16[1024,1792]{1,0:T(8,128)(2,1)} %refs_0_.1), channel_id=1, source_target_pairs={{0,1},{1,0},{2,3},{3,2},{4,5},{5,4},{6,7},{7,6},{8,9},{9,8},{10,11... | collective-permute-start | bytes 11010056 | tf_op jit(solution)/shard_map/ppermute | solution.py:320
  11.0 18.0 %collective-permute-start.2 = (bf16[112,1024]{1,0:T(8,128)(2,1)}, bf16[112,1024]{1,0:T(8,128)(2,1)}, u32[]{:S(2)}, u32[]{:S(2)}) collective-permute-start(bf16[112,1024]{1,0:T(8,128)(2,1)} %get-tuple-element.65), channel_id=1, source_target_pairs={{0,2},{4,0},{8,4},{12,8},{14,12},{10,14},{6,10},{2,6},{1,3},{5,1},... | collective-permute-start | bytes 688136 | tf_op jit(solution)/shard_map/ppermute | solution.py:273
  13.5 15.5 %collective-permute-start.1 = (bf16[112,1024]{1,0:T(8,128)(2,1)S(1)}, bf16[112,1024]{1,0:T(8,128)(2,1)}, u32[]{:S(2)}, u32[]{:S(2)}) collective-permute-start(bf16[112,1024]{1,0:T(8,128)(2,1)S(1)} %get-tuple-element.66), channel_id=1, source_target_pairs={{0,4},{4,8},{8,12},{12,14},{14,10},{10,6},{6,2},{2,0},{1,5},{5,9},... | collective-permute-start | bytes 688136 | tf_op jit(solution)/shard_map/ppermute | solution.py:273
  32.3 13.7 %collective-permute-start.4 = (bf16[224,1024]{1,0:T(8,128)(2,1)}, bf16[224,1024]{1,0:T(8,128)(2,1)S(1)}, u32[]{:S(2)}, u32[]{:S(2)}) collective-permute-start(bf16[224,1024]{1,0:T(8,128)(2,1)} %get-tuple-element.36), channel_id=1, source_target_pairs={{0,2},{4,0},{8,4},{12,8},{14,12},{10,14},{6,10},{2,6},{1,3},{5,1},... | collective-permute-start | bytes 1376264 | tf_op jit(solution)/shard_map/ppermute | solution.py:273
  34.3 13.7 %collective-permute-start.3 = (bf16[224,1024]{1,0:T(8,128)(2,1)}, bf16[224,1024]{1,0:T(8,128)(2,1)S(1)}, u32[]{:S(2)}, u32[]{:S(2)}) collective-permute-start(bf16[224,1024]{1,0:T(8,128)(2,1)} %get-tuple-element.35.refs_0_), channel_id=1, source_target_pairs={{0,4},{4,8},{8,12},{12,14},{14,10},{10,6},{6,2},{2,0},{1,5},{5,9},... | collective-permute-start | bytes 1376264 | tf_op jit(solution)/shard_map/ppermute | solution.py:273
  38.9 15.9 %collective-permute-start.10 = (bf16[224,896]{1,0:T(8,128)(2,1)}, bf16[224,896]{1,0:T(8,128)(2,1)S(1)}, u32[]{:S(2)}, u32[]{:S(2)}) collective-permute-start(bf16[224,896]{1,0:T(8,128)(2,1)} %get-tuple-element.40), channel_id=1, source_target_pairs={{0,2},{4,0},{8,4},{12,8},{14,12},{10,14},{6,10},{2,6},{1,3},{5,1},... | collective-permute-start | bytes 1204232 | tf_op jit(solution)/shard_map/ppermute | solution.py:273
  40.5 16.0 %collective-permute-start.9 = (bf16[224,896]{1,0:T(8,128)(2,1)}, bf16[224,896]{1,0:T(8,128)(2,1)S(1)}, u32[]{:S(2)}, u32[]{:S(2)}) collective-permute-start(bf16[224,896]{1,0:T(8,128)(2,1)} %get-tuple-element.37.refs_0_), channel_id=1, source_target_pairs={{0,4},{4,8},{8,12},{12,14},{14,10},{10,6},{6,2},{2,0},{1,5},{5,9},... | collective-permute-start | bytes 1204232 | tf_op jit(solution)/shard_map/ppermute | solution.py:273
  52.1 13.7 %collective-permute-start.8 = (bf16[224,1024]{1,0:T(8,128)(2,1)}, bf16[224,1024]{1,0:T(8,128)(2,1)S(1)}, u32[]{:S(2)}, u32[]{:S(2)}) collective-permute-start(bf16[224,1024]{1,0:T(8,128)(2,1)} %get-tuple-element.39), channel_id=1, source_target_pairs={{0,2},{4,0},{8,4},{12,8},{14,12},{10,14},{6,10},{2,6},{1,3},{5,1},... | collective-permute-start | bytes 1376264 | tf_op jit(solution)/shard_map/ppermute | solution.py:273
  53.7 13.7 %collective-permute-start.7 = (bf16[224,1024]{1,0:T(8,128)(2,1)}, bf16[224,1024]{1,0:T(8,128)(2,1)S(1)}, u32[]{:S(2)}, u32[]{:S(2)}) collective-permute-start(bf16[224,1024]{1,0:T(8,128)(2,1)} %get-tuple-element.38.refs_0_), channel_id=1, source_target_pairs={{0,4},{4,8},{8,12},{12,14},{14,10},{10,6},{6,2},{2,0},{1,5},{5,9},... | collective-permute-start | bytes 1376264 | tf_op jit(solution)/shard_map/ppermute | solution.py:273
  60.5 13.8 %collective-permute-start.14 = (bf16[224,896]{1,0:T(8,128)(2,1)}, bf16[224,896]{1,0:T(8,128)(2,1)S(1)}, u32[]{:S(2)}, u32[]{:S(2)}) collective-permute-start(bf16[224,896]{1,0:T(8,128)(2,1)} %get-tuple-element.44), channel_id=1, source_target_pairs={{0,2},{4,0},{8,4},{12,8},{14,12},{10,14},{6,10},{2,6},{1,3},{5,1},... | collective-permute-start | bytes 1204232 | tf_op jit(solution)/shard_map/ppermute | solution.py:273
  62.1 13.9 %collective-permute-start.13 = (bf16[224,896]{1,0:T(8,128)(2,1)}, bf16[224,896]{1,0:T(8,128)(2,1)S(1)}, u32[]{:S(2)}, u32[]{:S(2)}) collective-permute-start(bf16[224,896]{1,0:T(8,128)(2,1)} %get-tuple-element.41.refs_0_), channel_id=1, source_target_pairs={{0,4},{4,8},{8,12},{12,14},{14,10},{10,6},{6,2},{2,0},{1,5},{5,9},... | collective-permute-start | bytes 1204232 | tf_op jit(solution)/shard_map/ppermute | solution.py:273
  71.6 13.7 %collective-permute-start.12 = (bf16[224,1024]{1,0:T(8,128)(2,1)}, bf16[224,1024]{1,0:T(8,128)(2,1)S(1)}, u32[]{:S(2)}, u32[]{:S(2)}) collective-permute-start(bf16[224,1024]{1,0:T(8,128)(2,1)} %get-tuple-element.43), channel_id=1, source_target_pairs={{0,2},{4,0},{8,4},{12,8},{14,12},{10,14},{6,10},{2,6},{1,3},{5,1},... | collective-permute-start | bytes 1376264 | tf_op jit(solution)/shard_map/ppermute | solution.py:273
  73.2 13.7 %collective-permute-start.11 = (bf16[224,1024]{1,0:T(8,128)(2,1)}, bf16[224,1024]{1,0:T(8,128)(2,1)S(1)}, u32[]{:S(2)}, u32[]{:S(2)}) collective-permute-start(bf16[224,1024]{1,0:T(8,128)(2,1)} %get-tuple-element.42.refs_0_), channel_id=1, source_target_pairs={{0,4},{4,8},{8,12},{12,14},{14,10},{10,6},{6,2},{2,0},{1,5},{5,9},... | collective-permute-start | bytes 1376264 | tf_op jit(solution)/shard_map/ppermute | solution.py:273
  80.0 13.9 %collective-permute-start.18 = (bf16[224,896]{1,0:T(8,128)(2,1)}, bf16[224,896]{1,0:T(8,128)(2,1)S(1)}, u32[]{:S(2)}, u32[]{:S(2)}) collective-permute-start(bf16[224,896]{1,0:T(8,128)(2,1)} %get-tuple-element.46), channel_id=1, source_target_pairs={{0,2},{4,0},{8,4},{12,8},{14,12},{10,14},{6,10},{2,6},{1,3},{5,1},... | collective-permute-start | bytes 1204232 | tf_op jit(solution)/shard_map/ppermute | solution.py:273
  81.1 14.1 %collective-permute-start.17 = (bf16[224,896]{1,0:T(8,128)(2,1)}, bf16[224,896]{1,0:T(8,128)(2,1)S(1)}, u32[]{:S(2)}, u32[]{:S(2)}) collective-permute-start(bf16[224,896]{1,0:T(8,128)(2,1)} %get-tuple-element.45.refs_0_), channel_id=1, source_target_pairs={{0,4},{4,8},{8,12},{12,14},{14,10},{10,6},{6,2},{2,0},{1,5},{5,9},... | collective-permute-start | bytes 1204232 | tf_op jit(solution)/shard_map/ppermute | solution.py:273
  92.9 54.4 %collective-permute-start.33 = (bf16[224,1024]{1,0:T(8,128)(2,1)}, bf16[224,1024]{1,0:T(8,128)(2,1)S(1)}, u32[]{:S(2)}, u32[]{:S(2)}) collective-permute-start(bf16[224,1024]{1,0:T(8,128)(2,1)} %shard_map.36.refs_0_.refs_2_), channel_id=1, source_target_pairs={{0,1},{1,0},{2,3},{3,2},{4,5},{5,4},{6,7},{7,6},{8,9},{9,8},{10,11... | collective-permute-start | bytes 1376264 | tf_op jit(solution)/shard_map/ppermute | solution.py:325
  98.9 48.2 %collective-permute-start.42 = (bf16[224,896]{1,0:T(8,128)(2,1)}, bf16[224,896]{1,0:T(8,128)(2,1)S(1)}, u32[]{:S(2)}, u32[]{:S(2)}) collective-permute-start(bf16[224,896]{1,0:T(8,128)(2,1)} %shard_map.37.refs_2_.refs_11_), channel_id=1, source_target_pairs={{0,1},{1,0},{2,3},{3,2},{4,5},{5,4},{6,7},{7,6},{8,9},{9,8},{10,11... | collective-permute-start | bytes 1204232 | tf_op jit(solution)/shard_map/ppermute | solution.py:325
  99.0 12.4 %collective-permute-start.22 = (bf16[224,896]{1,0:T(8,128)(2,1)}, bf16[224,896]{1,0:T(8,128)(2,1)S(1)}, u32[]{:S(2)}, u32[]{:S(2)}) collective-permute-start(bf16[224,896]{1,0:T(8,128)(2,1)} %shard_map.37.refs_2_.refs_11_), channel_id=1, source_target_pairs={{0,2},{4,0},{8,4},{12,8},{14,12},{10,14},{6,10},{2,6},{1,3},{5,1},... | collective-permute-start | bytes 1204232 | tf_op jit(solution)/shard_map/ppermute | solution.py:273
  100.2 11.9 %collective-permute-start.21 = (bf16[224,896]{1,0:T(8,128)(2,1)}, bf16[224,896]{1,0:T(8,128)(2,1)}, u32[]{:S(2)}, u32[]{:S(2)}) collective-permute-start(bf16[224,896]{1,0:T(8,128)(2,1)} %shard_map.37.refs_2_.refs_11_), channel_id=1, source_target_pairs={{0,4},{4,8},{8,12},{12,14},{14,10},{10,6},{6,2},{2,0},{1,5},{5,9},... | collective-permute-start | bytes 1204232 | tf_op jit(solution)/shard_map/ppermute | solution.py:273
  101.7 19.0 %collective-permute-start.20 = (bf16[224,1024]{1,0:T(8,128)(2,1)}, bf16[224,1024]{1,0:T(8,128)(2,1)S(1)}, u32[]{:S(2)}, u32[]{:S(2)}) collective-permute-start(bf16[224,1024]{1,0:T(8,128)(2,1)} %get-tuple-element.48.refs_4_), channel_id=1, source_target_pairs={{0,2},{4,0},{8,4},{12,8},{14,12},{10,14},{6,10},{2,6},{1,3},{5,1},... | collective-permute-start | bytes 1376264 | tf_op jit(solution)/shard_map/ppermute | solution.py:273
  111.3 11.9 %collective-permute-start.19 = (bf16[224,1024]{1,0:T(8,128)(2,1)}, bf16[224,1024]{1,0:T(8,128)(2,1)S(1)}, u32[]{:S(2)}, u32[]{:S(2)}) collective-permute-start(bf16[224,1024]{1,0:T(8,128)(2,1)} %get-tuple-element.47.refs_2_.refs_3_), channel_id=1, source_target_pairs={{0,4},{4,8},{8,12},{12,14},{14,10},{10,6},{6,2},{2,0},{1,5},{5,9},... | collective-permute-start | bytes 1376264 | tf_op jit(solution)/shard_map/ppermute | solution.py:273
  112.1 35.7 %collective-permute-start.44 = (bf16[224,896]{1,0:T(8,128)(2,1)}, bf16[224,896]{1,0:T(8,128)(2,1)}, u32[]{:S(2)}, u32[]{:S(2)}) collective-permute-start(bf16[224,896]{1,0:T(8,128)(2,1)} %get-tuple-element.52.refs_13_), channel_id=1, source_target_pairs={{0,1},{1,0},{2,3},{3,2},{4,5},{5,4},{6,7},{7,6},{8,9},{9,8},{10,11... | collective-permute-start | bytes 1204232 | tf_op jit(solution)/shard_map/ppermute | solution.py:325
  131.8 11.4 %collective-permute-start.24 = (bf16[224,1024]{1,0:T(8,128)(2,1)}, bf16[224,1024]{1,0:T(8,128)(2,1)S(1)}, u32[]{:S(2)}, u32[]{:S(2)}) collective-permute-start(bf16[224,1024]{1,0:T(8,128)(2,1)} %get-tuple-element.51.refs_6_), channel_id=1, source_target_pairs={{0,2},{4,0},{8,4},{12,8},{14,12},{10,14},{6,10},{2,6},{1,3},{5,1},... | collective-permute-start | bytes 1376264 | tf_op jit(solution)/shard_map/ppermute | solution.py:273
  133.1 11.2 %collective-permute-start.23 = (bf16[224,1024]{1,0:T(8,128)(2,1)}, bf16[224,1024]{1,0:T(8,128)(2,1)S(1)}, u32[]{:S(2)}, u32[]{:S(2)}) collective-permute-start(bf16[224,1024]{1,0:T(8,128)(2,1)} %get-tuple-element.50.refs_2_.refs_5_), channel_id=1, source_target_pairs={{0,4},{4,8},{8,12},{12,14},{14,10},{10,6},{6,2},{2,0},{1,5},{5,9},... | collective-permute-start | bytes 1376264 | tf_op jit(solution)/shard_map/ppermute | solution.py:273
  (69 other events, 285.6 us)
